TPU v7x, 128 devices: a whole 4x4x4 slice. The times are simulated.
128 devices in a mesh: vec: 8 (over y, x_lo), walk: 16 (over x_hi, z, core).
Axes of the slice: x: 4 (x_hi: 2, x_lo: 2; x = x_hi * 2 + x_lo), y: 4, z: 4, core: 2. Of those that a mesh axis runs over, the one named last changes fastest.
Arguments:
- walkers: bfloat16 [256, 1024, 128], P('walk', 'vec'), may hold values from -6 to 6
- inverse: bfloat16 [256, 2, 2, 32, 32], P('walk'), may hold values from -0.75 to 0.75
- vectors: bfloat16 [10240, 1024, 128], P('walk', 'vec'), may hold values from -0.015625 to 0.015625
- sources: int32 [256], replicated, may hold values from 0 to 255
Outputs:
- moved: bfloat16 [256, 1024, 128], P('walk', 'vec')
- force_bias: float32 [2, 256, 10240], P(None, 'vec', 'walk')
Inputs may be any that keep to these rules, and one draw needn't show every extreme that they name: New walker j is a copy of old walker sources[j]; an old walker may be copied many times or not at all.
All inputs are finite; a program needn't handle non-finite values.
Results may differ from a plain program's by a relative error of at most 0.0029.
Values may be sent and summed in bfloat16 or wider, within the bound.
No kernel may reach another device: no remote copies, remote signals or barrier semaphores. Data moves between devices by JAX's collectives and lax.ppermute only.
A program may use at most 192 MiB of HBM per device.

v0:
```python
import jax
import jax.numpy as jnp
from jax import lax
from jax.sharding import PartitionSpec as P


def block_of(part):
    real_part, imag_part = (part[:, 0], part[:, 1])
    first = jnp.stack([real_part, imag_part], 3)
    second = jnp.stack([-imag_part, real_part], 3)
    return jnp.stack([first, second], 2)


def green(moved, moved_inverse):
    count, orbitals = (moved.shape[0], moved.shape[1])
    operator = block_of(moved_inverse)
    parts = moved.reshape(count, orbitals, 2, 2, -1)
    theta = jnp.einsum("wpcsk,wsckdi->wpdsi", parts, operator, preferred_element_type=jnp.float32)
    return theta.reshape(count, orbitals, -1).astype(jnp.bfloat16)


def rows_of(theta):
    count, orbitals = (theta.shape[0], theta.shape[1])
    split = theta.reshape(count, orbitals, 2, -1)
    first = jnp.stack([split[:, :, 0], -split[:, :, 1]], 2).reshape(count, -1)
    second = jnp.stack([split[:, :, 1], split[:, :, 0]], 2).reshape(count, -1)
    return jnp.stack([first, second], 0)


def bias_terms(theta, flat_vectors):
    count = theta.shape[0]
    stacked = rows_of(theta).reshape(2 * count, -1)
    product = lax.dot_general(
        stacked, flat_vectors, (((1,), (1,)), ((), ())), preferred_element_type=jnp.float32
    )
    return product.reshape(2, count, flat_vectors.shape[0])


def per_device(walkers, inverse, vectors, sources):
    cycle_index = lax.axis_index("walk")
    local_count = walkers.shape[0]
    flat_vectors = vectors.reshape(vectors.shape[0], -1)
    wanted = lax.dynamic_slice_in_dim(sources, cycle_index * local_count, local_count)
    piece_walk = lax.all_gather(walkers, "walk", axis=0, tiled=True)
    piece_inverse = lax.all_gather(inverse, "walk", axis=0, tiled=True)
    number = piece_walk.shape[0]
    picks = (wanted[:, None] == jnp.arange(number, dtype=jnp.int32)[None, :]).astype(jnp.bfloat16)
    new_walk = jnp.dot(picks, piece_walk.reshape(number, -1), preferred_element_type=jnp.float32)
    new_inverse = jnp.dot(
        picks, piece_inverse.reshape(number, -1), preferred_element_type=jnp.float32
    )
    moved = new_walk.astype(jnp.bfloat16).reshape(walkers.shape)
    moved_inverse = new_inverse.astype(jnp.bfloat16).reshape(inverse.shape)
    theta = green(moved, moved_inverse)
    partial_bias = bias_terms(lax.all_gather(theta, "walk", axis=0, tiled=True), flat_vectors)
    force_bias = lax.psum_scatter(partial_bias, "vec", scatter_dimension=1, tiled=True)
    return (moved, force_bias)


def solution(mesh):
    in_specs = (
        P("walk", "vec", None),
        P("walk", None, None, None, None),
        P("walk", "vec", None),
        P(),
    )
    out_specs = (P("walk", "vec", None), P(None, "vec", "walk"))
    return jax.shard_map(
        per_device, mesh=mesh, in_specs=in_specs, out_specs=out_specs, check_vma=False
    )
```

profile of v0, /device:TPU:0, one launch (start us, length us, event | category | flops | bytes accessed | tf_op | source)
XLA Modules:
  0.0 380.7 jit_solution(16915118415983859978)
XLA Ops:
  7.2 0.7 all-gather.6.cloned.1.call-update
  7.9 0.7 all-gather.4.cloned.1.call-update
  8.7 0.8 dynamic_slice.3
  9.5 76.6 %all-gather.6.cloned.1.call-done = bf16[256,2,2,32,32]{4,3,2,1,0:T(8,128)(2,1)} async-done(((bf16[16,2,2,32,32]{4,3,2,1,0:T(8,128)(2,1)}), bf16[256,2,2,32,32]{4,3,2,1,0:T(8,128)(2,1)}) %all-gather.6.cloned.1.call-update) | async-done | bytes 2097168 | tf_op jit(solution)/shard_map/all_gather | solution.py:45
  86.1 9.1 %copy.20 = bf16[256,2,2,32,32]{0,4,3,2,1:T(8,128)(2,1)S(1)} copy(bf16[256,2,2,32,32]{4,3,2,1,0:T(8,128)(2,1)} %all-gather.6.cloned.1.call-done) | data formatting | bytes 4194304 | tf_op jit(solution)/shard_map/all_gather | solution.py:45
  95.2 0.6 convolution_convert_fusion.1
  96.7 1.0 maximum_bitcast_fusion
  97.7 61.7 %all-gather.4.cloned.1.call-done = bf16[256,128,128]{2,1,0:T(8,128)(2,1)} async-done(((bf16[16,128,128]{2,1,0:T(8,128)(2,1)}), bf16[256,128,128]{2,1,0:T(8,128)(2,1)}) %all-gather.4.cloned.1.call-update) | async-done | bytes 8388624 | tf_op jit(solution)/shard_map/all_gather | solution.py:44
  159.4 7.9 %convolution_convert_fusion = bf16[16,16384]{1,0:T(8,128)(2,1)S(1)} fusion(bf16[32,8,128,128]{3,2,1,0:T(8,128)(2,1)} %bitcast.36, s32[16]{0:T(128)S(1)} %dynamic_slice.3), kind=kOutput, calls=%fused_computation | convolution fusion | flops 134483968 | bytes 8912960 | tf_op jit(solution)/shard_map/dot_general | solution.py:48
  167.3 1.6 reshape_reshape.3
  168.9 1.9 fusion.14
  170.9 1.0 copy.26
  172.1 31.4 %reshape.47 = bf16[640,16384,1]{1,0,2:T(8,128)(2,1)} reshape(bf16[640,128,128]{2,1,0:T(8,128)(2,1)} %param.6) | data formatting | bytes 41943040 | tf_op jit(solution)/shard_map/reshape | solution.py:42
  203.5 39.3 %all-gather.8.cloned.1.call-done = bf16[256,128,128]{2,1,0:T(8,128)(2,1)} async-done(((bf16[16,128,128]{2,1,0:T(8,128)(2,1)}), bf16[256,128,128]{2,1,0:T(8,128)(2,1)}) %all-gather.8.cloned.1.call-update) | async-done | bytes 8388624 | tf_op jit(solution)/shard_map/all_gather | solution.py:55
  242.9 11.9 %copy.27 = bf16[256,128,128]{1,2,0:T(8,128)(2,1)} copy(bf16[256,128,128]{2,1,0:T(8,128)(2,1)} %all-gather.8.cloned.1.call-done) | data formatting | bytes 16777216 | tf_op jit(solution)/shard_map/all_gather | solution.py:55
  254.8 4.1 %slice_negate_fusion = (bf16[256,128,1,64]{1,3,2,0:T(8,128)(2,1)S(1)}, bf16[256,128,1,64]{1,3,2,0:T(8,128)(2,1)S(1)}, bf16[256,128,1,64]{1,3,2,0:T(8,128)(2,1)S(1)}) fusion(bf16[256,128,2,64]{1,3,2,0:T(8,128)(2,1)} %bitcast.32), kind=kLoop, calls=%fused_computation.26 | loop fusion | flops 2097152 | bytes 20971520 | tf_op jit(solution)/shard_map/neg | solution.py:25
  258.8 6.1 %pad_maximum_fusion = (bf16[256,128,2,64]{1,3,2,0:T(8,128)(2,1)}, bf16[256,128,2,64]{1,3,2,0:T(8,128)(2,1)}) fusion(bf16[256,128,1,64]{1,3,2,0:T(8,128)(2,1)S(1)} %get-tuple-element.2, bf16[256,128,1,64]{1,3,2,0:T(8,128)(2,1)S(1)} %get-tuple-element.4, bf16[256,128,1,64]{1,3,2,0:T(8,128)(2,1)S(1)} %get-tuple-element.3), kind=kLoop, calls=%fused_computation.7 | loop fusion | flops 8388608 | bytes 29360128 | tf_op jit(solution)/shard_map/stack | solution.py:25
  265.0 13.5 %copy.28 = bf16[256,128,2,64]{0,3,2,1:T(8,128)(2,1)} copy(bf16[256,128,2,64]{1,3,2,0:T(8,128)(2,1)} %get-tuple-element.5) | data formatting | bytes 16777216 | tf_op jit(solution)/shard_map/stack | solution.py:25
  278.4 11.9 %copy.30 = bf16[1,256,16384]{2,1,0:T(8,128)(2,1)} copy(bf16[1,256,16384]{1,2,0:T(8,128)(2,1)} %bitcast.33) | data formatting | bytes 16777216 | tf_op jit(solution)/shard_map/stack;reshape | solution.py:27
  290.4 13.5 %copy.29 = bf16[256,128,2,64]{0,3,2,1:T(8,128)(2,1)} copy(bf16[256,128,2,64]{1,3,2,0:T(8,128)(2,1)} %get-tuple-element.6) | data formatting | bytes 16777216 | tf_op jit(solution)/shard_map/stack | solution.py:26
  303.8 11.8 %copy.31 = bf16[1,256,16384]{2,1,0:T(8,128)(2,1)} copy(bf16[1,256,16384]{1,2,0:T(8,128)(2,1)} %bitcast.34) | data formatting | bytes 16777216 | tf_op jit(solution)/shard_map/stack;reshape | solution.py:27
  315.6 18.9 %fusion = f32[2,256,640]{2,1,0:T(8,128)} fusion(bf16[640,16384,1]{1,0,2:T(8,128)(2,1)} %reshape.47, bf16[1,256,16384]{2,1,0:T(8,128)(2,1)} %copy.31, bf16[1,256,16384]{2,1,0:T(8,128)(2,1)} %copy.30), kind=kOutput, calls=%fused_computation.1 | convolution fusion | flops 10745806848 | bytes 39059456 | tf_op jit(solution)/shard_map/dot_general | solution.py:33
  334.6 0.9 copy.39
  335.5 38.7 %reduce-scatter.2.cloned.1.call-done = f32[2,32,640]{2,1,0:T(8,128)} async-done(((f32[2,256,640]{2,1,0:T(8,128)}), f32[2,32,640]{2,1,0:T(8,128)}) %reduce-scatter.2.cloned.1.call-update) | async-done | bytes 163856 | tf_op jit(solution)/shard_map/reduce_scatter | solution.py:56
  (12 shorter events, 1.2 us)
Async XLA Ops:
  7.2 78.9 %all-gather.6.cloned.1.call-start = ((), (), s32[]{:S(2)}) async-start(), calls=%async_computation.2 | async-start | bytes 8912896 | tf_op jit(solution)/shard_map/all_gather | solution.py:45
  7.9 151.5 %all-gather.4.cloned.1.call-start = ((), (), s32[]{:S(2)}) async-start(), calls=%async_computation.1 | async-start | bytes 8912896 | tf_op jit(solution)/shard_map/all_gather | solution.py:44
  8.6 234.2 %all-gather.8.cloned.1.call-start = ((), (), s32[]{:S(2)}) async-start(), calls=%async_computation.3 | async-start | bytes 8912896 | tf_op jit(solution)/shard_map/all_gather | solution.py:55
  171.9 202.3 %reduce-scatter.2.cloned.1.call-start = ((), (), s32[]{:S(2)}) async-start(), calls=%async_computation.4 | async-start | bytes 1474560 | tf_op jit(solution)/shard_map/reduce_scatter | solution.py:56
Sparse Core Ops, SparseCore 0:
  10.5 75.5 all-gather.5
  88.6 70.8 all-gather.3
  172.0 70.8 all-gather.7
  334.7 39.4 reduce-scatter.1
where the time goes:
time: 383 us; the launch traced here: 381 us
  waiting for transfers between devices  218 us (57%)
  local copies, waits for them, and re-layouts  108 us (28%)
  matrix products  29.3 us (8%)
  between operations  13.8 us (4%)
  other arithmetic  11.2 us (3%)
    all_gather x1, waiting for transfers between devices, per_device(): piece_inverse = lax.all_gather(inverse, 'walk', axis=0, tiled=True)  76.6 us
    all_gather x1, waiting for transfers between devices, per_device(): piece_walk = lax.all_gather(walkers, 'walk', axis=0, tiled=True)  61.7 us
    all_gather x1, waiting for transfers between devices, per_device(): lax.all_gather(theta, 'walk', axis=0, tiled=True)  39.3 us
    reduce_scatter x1, waiting for transfers between devices, per_device(): lax.psum_scatter(partial_bias, 'vec', scatter_dimension=1, tiled=True)  38.7 us
    reshape x1, local copies, waits for them, and re-layouts, per_device(): flat_vectors = vectors.reshape(vectors.shape[0], -1)  31.4 us
    another operation x2, local copies, waits for them, and re-layouts, rows_of(): return jnp.stack([first, second], 0)  23.7 us
    dot_general x1, matrix products, bias_terms(): lax.dot_general(stacked, flat_vectors, (((1,), (1,)), ((), ())), preferre...  18.9 us
    another operation x1, local copies, waits for them, and re-layouts, rows_of(): first = jnp.stack([split[:, :, 0], -split[:, :, 1]], 2).reshape(count, -1)  13.5 us
  transfers between devices with their start and end apart: 4, of which 4 were waited for; matrix products, arithmetic and copies ran while one was open for 12% of the time, Pallas kernels for 0%

commit v1 on v0

v1 whole, which is shorter than its diff:
```python
import functools

import jax
import jax.numpy as jnp
from jax import lax
from jax.experimental import pallas as pl
from jax.experimental.pallas import tpu as pltpu
from jax.sharding import PartitionSpec as P

BF = jnp.bfloat16
F32 = jnp.float32


def swap_matrix():
    row = lax.broadcasted_iota(jnp.int32, (256, 256), 0)
    col = lax.broadcasted_iota(jnp.int32, (256, 256), 1)
    hit = (row // 16 == col % 16) & (row % 16 == col // 16)
    return jnp.where(hit, 1.0, 0.0).astype(BF)


def flatten_kernel(v_ref, out_ref):
    swap = swap_matrix()
    for p in range(0, 128, 16):
        pair = [v_ref[g : g + 16, p : p + 16, :].reshape(256, 128) for g in (0, 16)]
        both = jnp.dot(swap, jnp.concatenate(pair, axis=1), preferred_element_type=F32)
        both = both.astype(BF)
        for q in range(16):
            for h in range(2):
                out_ref[h * 16 : h * 16 + 16, (p + q) * 128 : (p + q + 1) * 128] = both[
                    q * 16 : q * 16 + 16, h * 128 : h * 128 + 128
                ]


def flatten_vectors(vectors):
    count = vectors.shape[0]
    return pl.pallas_call(
        flatten_kernel,
        grid=(count // 32,),
        in_specs=[pl.BlockSpec((32, 128, 128), lambda i: (i, 0, 0))],
        out_specs=pl.BlockSpec((32, 16384), lambda i: (i, 0)),
        out_shape=jax.ShapeDtypeStruct((count, 16384), BF),
        compiler_params=pltpu.CompilerParams(vmem_limit_bytes=32 << 20),
        cost_estimate=pl.CostEstimate(
            flops=2 * count * 16384 * 256, bytes_accessed=4 * count * 16384, transcendentals=0
        ),
    )(vectors)


def theta_kernel(split, *refs):
    out_ref, work = refs[-2:]
    refs = refs[:-2]
    swap = swap_matrix()
    lane = lax.broadcasted_iota(jnp.int32, (32, 128), 1)
    sign = jnp.where(lane < 64, 1.0, -1.0)
    keep0 = jnp.where(lane % 64 < 32, 1.0, 0.0)
    keep1 = 1.0 - keep0

    def walker(ref, w, slot):
        small = ref[w, 128:160, :].astype(F32)
        a = small * sign
        b = jnp.concatenate([small[:, 64:], small[:, :64]], axis=1)
        ab = jnp.concatenate([a, b], axis=1)
        ba = jnp.concatenate([-b, a], axis=1)
        k0 = jnp.concatenate([keep0, keep0], axis=1)
        k1 = jnp.concatenate([keep1, keep1], axis=1)
        operator = jnp.concatenate([ab * k0, ab * k1, ba * k0, ba * k1], axis=0).astype(BF)
        work[slot] = jnp.dot(ref[w, 0:128, :], operator, preferred_element_type=F32).astype(BF)

    per = 2 if split else 1
    for half in range(2):
        for n in range(per):
            ref = refs[half * per + n]
            size = 16 // per

            @pl.loop(0, size, unroll=2)
            def _(w):
                walker(ref, w, n * size + w)

        for p in range(0, 128, 16):
            turned = jnp.dot(
                swap, work[:, p : p + 16, :].reshape(256, 256), preferred_element_type=F32
            ).astype(BF)
            for q in range(16):
                for c in range(2):
                    row = c * 32 + half * 16
                    out_ref[row : row + 16, (p + q) * 128 : (p + q + 1) * 128] = turned[
                        q * 16 : q * 16 + 16, c * 128 : c * 128 + 128
                    ]


def theta_of(*pieces):
    return pl.pallas_call(
        functools.partial(theta_kernel, len(pieces) == 4),
        out_shape=jax.ShapeDtypeStruct((64, 16384), BF),
        scratch_shapes=[pltpu.VMEM((16, 128, 256), BF)],
        compiler_params=pltpu.CompilerParams(vmem_limit_bytes=32 << 20),
        cost_estimate=pl.CostEstimate(
            flops=2 * 32 * 16384 * 256 * 2, bytes_accessed=6 << 20, transcendentals=0
        ),
    )(*pieces)


def product_kernel(last, v_ref, *refs):
    thetas = refs[:4]
    pick_ref = refs[4]
    rest = refs[5:]
    acc = rest[-1]
    step = pl.program_id(0)

    @pl.when(step == 0)
    def _():
        acc[...] = jnp.zeros_like(acc)

    theta = jnp.concatenate([t[...] for t in thetas], axis=0)
    acc[...] += lax.dot_general(
        v_ref[...], theta, (((1,), (1,)), ((), ())), preferred_element_type=F32
    )

    @pl.when(step == pl.num_programs(0) - 1)
    def _():
        bias = acc[...].astype(BF)
        picked = lax.dot_general(
            pick_ref[...], bias, (((1,), (1,)), ((), ())), preferred_element_type=F32
        )
        if last:
            rest[1][...] = (picked + rest[0][...]).astype(BF)
        else:
            rest[0][...] = picked


def product(flat, thetas, pick, before=None):
    count = flat.shape[0]
    depth = 1024
    last = before is not None
    extra = [before] if last else []
    whole = lambda shape: pl.BlockSpec(shape, lambda k: (0, 0))
    return pl.pallas_call(
        functools.partial(product_kernel, last),
        grid=(16384 // depth,),
        in_specs=[pl.BlockSpec((count, depth), lambda k: (0, k))]
        + [pl.BlockSpec((64, depth), lambda k: (0, k))] * 4
        + [whole((512, 256))]
        + [whole((512, count))] * len(extra),
        out_specs=whole((512, count)),
        out_shape=jax.ShapeDtypeStruct((512, count), BF if last else F32),
        scratch_shapes=[pltpu.VMEM((count, 256), F32)],
        compiler_params=pltpu.CompilerParams(vmem_limit_bytes=32 << 20),
        cost_estimate=pl.CostEstimate(
            flops=2 * count * 16384 * 256, bytes_accessed=2 * (count + 256) * 16384, transcendentals=0
        ),
    )(flat, *thetas, pick, *extra)


def moved_kernel(sizes, piece_ref, row_ref, *refs):
    sources, out_ref, sem = refs[:-2], refs[-2], refs[-1]
    for j in range(16):
        for n, src in enumerate(sources):

            @pl.when(piece_ref[j] == n)
            def _(j=j, src=src):
                pltpu.make_async_copy(
                    src.at[row_ref[j], pl.ds(0, 128), :], out_ref.at[j], sem.at[j]
                ).start()

    for j in range(16):
        pltpu.make_async_copy(
            sources[0].at[0, pl.ds(0, 128), :], out_ref.at[j], sem.at[j]
        ).wait()


def moved_of(piece, row, pieces):
    sizes = tuple(p.shape[0] for p in pieces)
    return pl.pallas_call(
        functools.partial(moved_kernel, sizes),
        grid_spec=pltpu.PrefetchScalarGridSpec(
            num_scalar_prefetch=2,
            grid=(1,),
            in_specs=[pl.BlockSpec(memory_space=pl.ANY)] * len(pieces),
            out_specs=pl.BlockSpec(memory_space=pl.ANY),
            scratch_shapes=[pltpu.SemaphoreType.DMA((16,))],
        ),
        out_shape=jax.ShapeDtypeStruct((16, 128, 128), BF),
    )(piece, row, *pieces)


def index(x, z, core):
    return (x % 2 * 4 + z % 4) * 2 + core


def moves(step):
    return [
        (index(x, z, c), index(*step(x, z, c))) for x in range(2) for z in range(4) for c in range(2)
    ]


ACROSS = moves(lambda x, z, c: (x + 1, z, c))
UP = moves(lambda x, z, c: (x, z + 1, c))
DOWN = moves(lambda x, z, c: (x, z - 1, c))
OTHER = moves(lambda x, z, c: (x, z, 1 - c))


def send(value, pairs):
    return lax.ppermute(value, "walk", pairs)


def per_device(walkers, inverse, vectors, sources):
    me = lax.axis_index("walk")
    x, z, core = me // 8, me // 2 % 4, me % 2
    small = inverse.transpose(0, 3, 1, 2, 4).reshape(16, 32, 128)
    own = jnp.concatenate([walkers, small], axis=1)
    across = send(own, ACROSS)
    below = send(own, UP)
    above = send(own, DOWN)
    far0 = send(below[:8], UP)
    far1 = send(above[8:], DOWN)
    across_below = send(across, UP)
    across_above = send(across, DOWN)
    across_far0 = send(far0, ACROSS)
    across_far1 = send(far1, ACROSS)

    groups = [
        (0, 0, [own]),
        (1, 0, [across]),
        (0, -1, [below]),
        (0, 1, [above]),
        (0, 2, [far0, far1]),
        (1, -1, [across_below]),
        (1, 1, [across_above]),
        (1, 2, [across_far0, across_far1]),
    ]
    flat = flatten_vectors(vectors)
    old_ids, thetas, pieces, places = [], [], [], []
    sixteen = jnp.arange(16, dtype=jnp.int32)
    for dx, dz, parts in groups:
        both = parts + [send(part, OTHER) for part in parts]
        thetas.append(theta_of(*both))
        ids = []
        for c in (core, 1 - core):
            ids.append(index(x + dx, z + dz, c) * 16 + sixteen)
        old_ids.append(jnp.concatenate(ids))
        per = len(parts)
        base = len(pieces)
        for half in range(2):
            places.append(base + half * per + sixteen * per // 16)
        pieces += both
    vec = lax.axis_index("vec")
    targets = [((vec // 2 + dy) % 4) * 2 + (vec % 2 + dv) % 2 for dy in range(4) for dv in range(2)]
    wanted = jnp.stack([lax.dynamic_slice_in_dim(sources, t * 32, 32) for t in targets])
    picks = []
    for part in range(2):
        ids = jnp.stack(old_ids[4 * part : 4 * part + 4])
        same = wanted[:, None, :, None, None, None] == ids[None, None, None, :, None, :]
        kind = jnp.arange(2)
        same = same & (kind[None, :, None, None, None, None] == kind[None, None, None, None, :, None])
        picks.append(same.astype(BF).reshape(512, 256))
    first = product(flat, thetas[:4], picks[0])
    sums = product(flat, thetas[4:], picks[1], first)

    total = sums[:64].astype(F32)
    for n in range(1, 8):
        dy, dv = n // 2, n % 2
        pairs = [
            (y * 2 + v, ((y + dy) % 4) * 2 + (v + dv) % 2) for y in range(4) for v in range(2)
        ]
        total = total + lax.ppermute(sums[64 * n : 64 * n + 64], "vec", pairs).astype(F32)

    mine = lax.dynamic_slice_in_dim(sources, me * 16, 16)
    table = jnp.concatenate(old_ids)
    slot = jnp.argmax(mine[:, None] == table[None, :], axis=1).astype(jnp.int32)
    piece = jnp.concatenate(places)[slot]
    long = [p.shape[0] for p in pieces]
    row = slot % jnp.asarray(long, jnp.int32)[piece]
    moved = moved_of(piece, row, pieces)
    return (moved, total.reshape(2, 32, -1))


def solution(mesh):
    in_specs = (
        P("walk", "vec", None),
        P("walk", None, None, None, None),
        P("walk", "vec", None),
        P(),
    )
    out_specs = (P("walk", "vec", None), P(None, "vec", "walk"))
    return jax.shard_map(
        per_device, mesh=mesh, in_specs=in_specs, out_specs=out_specs, check_vma=False
    )
```

time: 383 us -> 190 us (0.50)
  waiting for transfers between devices: 218 us -> 6.96 us
  Pallas kernels: 0 us -> 114 us
  local copies, waits for them, and re-layouts: 108 us -> 21.8 us
  starting transfers between devices: 0.34 us -> 32.4 us
  matrix products: 29.3 us -> 0 us
  between operations: 13.8 us -> 1.2 us
    all_gather x3 -> x0, waiting for transfers between devices: 178 us -> none  [the longest x1 76.6 us: per_device(): piece_inverse = lax.all_gather(inverse, 'walk', axis=0, tiled=True)]
    pallas_call x0 -> x12, Pallas kernels: none -> 114 us  [the longest x8 45 us: theta_of(): pl.pallas_call(functools.partial(theta_kernel, len(pieces) == 4), out_sha...]
    another operation x5 -> x2, local copies, waits for them, and re-layouts: 52.3 us -> 0.13 us  [per_device(): jnp.stack([lax.dynamic_slice_in_dim(sources, t * 32, 32) for t in targets])]
    reduce_scatter x1 -> x0, waiting for transfers between devices: 38.7 us -> none  [per_device(): lax.psum_scatter(partial_bias, 'vec', scatter_dimension=1, tiled=True)]
    ppermute x0 -> x26, starting transfers between devices: none -> 32.4 us  [the longest x19 21 us: send(): return lax.ppermute(value, 'walk', pairs)]
    reshape x2 -> x1, local copies, waits for them, and re-layouts: 31.8 us -> 0.29 us  [per_device(): small = inverse.transpose(0, 3, 1, 2, 4).reshape(16, 32, 128)]
    dot_general x4 -> x0, matrix products: 29.3 us -> none  [the longest x1 18.9 us: bias_terms(): lax.dot_general(stacked, flat_vectors, (((1,), (1,)), ((), ())), preferre...]
    all_gather x2 -> x0, local copies, waits for them, and re-layouts: 21 us -> none  [the longest x1 11.9 us: per_device(): lax.all_gather(theta, 'walk', axis=0, tiled=True)]
  transfers between devices with their start and end apart: 4 -> 26, of which waited for: 4 -> 2; matrix products, arithmetic and copies ran while one was open for 12% -> 12% of each run, Pallas kernels for 0% -> 49%
where the time goes in v1:
time: 190 us; the launch traced here: 189 us
  Pallas kernels  114 us (60%)
  starting transfers between devices  32.4 us (17%)
  local copies, waits for them, and re-layouts  21.8 us (11%)
  other arithmetic  12.2 us (6%)
  waiting for transfers between devices  6.96 us (4%)
    pallas_call x8, Pallas kernels, theta_of(): pl.pallas_call(functools.partial(theta_kernel, len(pieces) == 4), out_sha...  45 us
    pallas_call x2, Pallas kernels, product(): pl.pallas_call(functools.partial(product_kernel, last), grid=(16384 // de...  33.4 us
    ppermute x19, starting transfers between devices, send(): return lax.ppermute(value, 'walk', pairs)  21 us
    pallas_call x1, Pallas kernels, flatten_vectors(): pl.pallas_call(flatten_kernel, grid=(count // 32,), in_specs=[pl.BlockSpe...  17.9 us
    pallas_call x1, Pallas kernels, moved_of(): pl.pallas_call(functools.partial(moved_kernel, sizes), grid_spec=pltpu.Pr...  17.8 us
    ppermute x7, starting transfers between devices, per_device(): lax.ppermute(sums[64 * n:64 * n + 64], 'vec', pairs).astype(F32)  11.4 us
    unnamed x39, local copies, waits for them, and re-layouts  8.86 us
    convert_element_type x2, local copies, waits for them, and re-layouts, per_device(): picks.append(same.astype(BF).reshape(512, 256))  7.74 us
  transfers between devices with their start and end apart: 26, of which 2 were waited for; matrix products, arithmetic and copies ran while one was open for 12% of the time, Pallas kernels for 49%

profile of v1, /device:TPU:0, one launch (start us, length us, event | category | flops | bytes accessed | tf_op | source)
XLA Modules:
  0.0 188.7 jit_solution(6796991091152141140)
XLA Ops:
  3.6 4.2 %collective-permute-start.5 = (bf16[16,160,128]{2,1,0:T(8,128)(2,1)S(1)}, bf16[16,160,128]{2,1,0:T(8,128)(2,1)S(1)}, u32[]{:S(2)}, u32[]{:S(2)}) collective-permute-start(bf16[16,160,128]{2,1,0:T(8,128)(2,1)S(1)} %constant_dynamic-update-slice_fusion.refs_0_), channel_id=1, source_target_pairs={{0,6},{1,7},{2,0},{3,1},{4,2},{5,3},{6,4},{7,5},{8,14},{9,15},{10,... | collective-permute-start | bytes 1966088 | tf_op jit(solution)/shard_map/ppermute | solution.py:203
  7.8 3.0 %collective-permute-start.1 = (bf16[16,160,128]{2,1,0:T(8,128)(2,1)S(1)}, bf16[16,160,128]{2,1,0:T(8,128)(2,1)S(1)}, u32[]{:S(2)}, u32[]{:S(2)}) collective-permute-start(bf16[16,160,128]{2,1,0:T(8,128)(2,1)S(1)} %constant_dynamic-update-slice_fusion.refs_0_), channel_id=1, source_target_pairs={{0,8},{1,9},{2,10},{3,11},{4,12},{5,13},{6,14},{7,15},{8,0},{9,1},... | collective-permute-start | bytes 1966088 | tf_op jit(solution)/shard_map/ppermute | solution.py:203
  16.4 5.4 %collective-permute-done.5.refs_6_.refs_0_ = bf16[16,160,128]{2,1,0:T(8,128)(2,1)S(1)} collective-permute-done((bf16[16,160,128]{2,1,0:T(8,128)(2,1)S(1)}, bf16[16,160,128]{2,1,0:T(8,128)(2,1)S(1)}, u32[]{:S(2)}, u32[]{:S(2)}) %collective-permute-start.5) | collective-permute-done | bytes 655392 | tf_op jit(solution)/shard_map/ppermute | solution.py:203
  21.8 3.8 %collective-permute-start.8 = (bf16[8,160,128]{2,1,0:T(8,128)(2,1)S(1)}, bf16[8,160,128]{2,1,0:T(8,128)(2,1)}, u32[]{:S(2)}, u32[]{:S(2)}) collective-permute-start(bf16[8,160,128]{2,1,0:T(8,128)(2,1)S(1)} %slice.45), channel_id=1, source_target_pairs={{0,6},{1,7},{2,0},{3,1},{4,2},{5,3},{6,4},{7,5},{8,14},{9,15},{10,... | collective-permute-start | bytes 983048 | tf_op jit(solution)/shard_map/ppermute | solution.py:203
  25.6 3.7 %and_convert_fusion = (bf16[8,2,32,4,2,32]{5,4,3,2,1,0:T(2,128)(2,1)}, bf16[8,2,32,4,2,32]{5,4,3,2,1,0:T(2,128)(2,1)}) fusion(pred[8,32,4,32]{3,2,1,0:T(4,128)(4,1)S(1)} %get-tuple-element.11, pred[2,2]{1,0:T(4,128)(4,1)S(1)} %iota_compare_fusion, pred[8,32,4,32]{3,2,1,0:T(4,128)(4,1)S(1)} %get-tuple-element.12), kind=kLoop, calls=%fused_computation.2 | loop fusion | flops 524288 | bytes 589828 | tf_op jit(solution)/shard_map/convert_element_type | solution.py:255
  31.7 3.0 %collective-permute-start.16 = (bf16[8,160,128]{2,1,0:T(8,128)(2,1)}, bf16[8,160,128]{2,1,0:T(8,128)(2,1)}, u32[]{:S(2)}, u32[]{:S(2)}) collective-permute-start(bf16[8,160,128]{2,1,0:T(8,128)(2,1)} %collective-permute-done.8.refs_9_.refs_1_), channel_id=1, source_target_pairs={{0,8},{1,9},{2,10},{3,11},{4,12},{5,13},{6,14},{7,15},{8,0},{9,1},... | collective-permute-start | bytes 983048 | tf_op jit(solution)/shard_map/ppermute | solution.py:203
  35.8 3.8 %collective-permute-start.13 = (bf16[16,160,128]{2,1,0:T(8,128)(2,1)S(1)}, bf16[16,160,128]{2,1,0:T(8,128)(2,1)}, u32[]{:S(2)}, u32[]{:S(2)}) collective-permute-start(bf16[16,160,128]{2,1,0:T(8,128)(2,1)S(1)} %collective-permute-done.1.refs_2_.refs_0_), channel_id=1, source_target_pairs={{0,6},{1,7},{2,0},{3,1},{4,2},{5,3},{6,4},{7,5},{8,14},{9,15},{10,... | collective-permute-start | bytes 1966088 | tf_op jit(solution)/shard_map/ppermute | solution.py:203
  40.2 4.2 %reshape.69.refs_4_ = bf16[512,256]{1,0:T(8,128)(2,1)} reshape(bf16[8,2,32,4,2,32]{5,4,3,2,1,0:T(2,128)(2,1)} %get-tuple-element.21) | data formatting | bytes 524288 | tf_op jit(solution)/shard_map/convert_element_type | solution.py:255
  44.4 3.6 %reshape.68.refs_4_ = bf16[512,256]{1,0:T(8,128)(2,1)S(1)} reshape(bf16[8,2,32,4,2,32]{5,4,3,2,1,0:T(2,128)(2,1)} %get-tuple-element.22) | data formatting | bytes 524288 | tf_op jit(solution)/shard_map/convert_element_type | solution.py:255
  50.4 17.9 %shard_map.69.v_ref = bf16[640,16384]{1,0:T(8,128)(2,1)S(1)} custom-call(bf16[640,128,128]{2,1,0:T(8,128)(2,1)} %v_ref.1), custom_call_target="tpu_custom_call" | custom-call | flops 5368709120 | bytes 41943040 | tf_op jit(solution)/shard_map/pallas_call | solution.py:36
  68.3 7.0 %copy-done = bf16[640,16384]{1,0:T(8,128)(2,1)} copy-done((bf16[640,16384]{1,0:T(8,128)(2,1)}, bf16[640,16384]{1,0:T(8,128)(2,1)S(1)}, u32[]{:S(2)}) %copy-start) | copy-done | bytes 20971544
  76.3 4.9 %shard_map.74.refs_0_ = bf16[64,16384]{1,0:T(8,128)(2,1)S(1)} custom-call(bf16[16,160,128]{2,1,0:T(8,128)(2,1)S(1)} %constant_dynamic-update-slice_fusion.refs_0_, bf16[16,160,128]{2,1,0:T(8,128)(2,1)S(1)} %collective-permute-done.refs_1_), custom_call_target="tpu_custom_call" | custom-call | flops 536870912 | bytes 6291456 | tf_op jit(solution)/shard_map/pallas_call | solution.py:92
  81.3 6.0 %shard_map.77.refs_3_ = bf16[64,16384]{1,0:T(8,128)(2,1)S(1)} custom-call(bf16[16,160,128]{2,1,0:T(8,128)(2,1)S(1)} %collective-permute-done.5.refs_6_.refs_0_, bf16[16,160,128]{2,1,0:T(8,128)(2,1)} %collective-permute-done.6.refs_7_.refs_1_), custom_call_target="tpu_custom_call" | custom-call | flops 536870912 | bytes 6291456 | tf_op jit(solution)/shard_map/pallas_call | solution.py:92
  87.9 6.0 %shard_map.76.refs_2_ = bf16[64,16384]{1,0:T(8,128)(2,1)S(1)} custom-call(bf16[16,160,128]{2,1,0:T(8,128)(2,1)S(1)} %collective-permute-done.3.refs_4_.refs_0_, bf16[16,160,128]{2,1,0:T(8,128)(2,1)} %collective-permute-done.4.refs_5_.refs_1_), custom_call_target="tpu_custom_call" | custom-call | flops 536870912 | bytes 6291456 | tf_op jit(solution)/shard_map/pallas_call | solution.py:92
  94.1 4.9 %shard_map.75.refs_1_ = bf16[64,16384]{1,0:T(8,128)(2,1)S(1)} custom-call(bf16[16,160,128]{2,1,0:T(8,128)(2,1)S(1)} %collective-permute-done.1.refs_2_.refs_0_, bf16[16,160,128]{2,1,0:T(8,128)(2,1)S(1)} %collective-permute-done.2.refs_3_.refs_1_), custom_call_target="tpu_custom_call" | custom-call | flops 536870912 | bytes 6291456 | tf_op jit(solution)/shard_map/pallas_call | solution.py:92
  99.6 6.0 %shard_map.70.refs_0_ = bf16[64,16384]{1,0:T(8,128)(2,1)S(1)} custom-call(bf16[8,160,128]{2,1,0:T(8,128)(2,1)} %collective-permute-done.7.refs_8_.refs_0_, bf16[8,160,128]{2,1,0:T(8,128)(2,1)} %collective-permute-done.8.refs_9_.refs_1_, bf16[8,160,128]{2,1,0:T(8,128)(2,1)S(1)} %collective-permute-done.9.refs_10_.refs_2_, ...), custom_call_target="tpu_custom_call" | custom-call | flops 536870912 | bytes 6291456 | tf_op jit(solution)/shard_map/pallas_call | solution.py:92
  106.4 16.7 %shard_map.78.refs_5_ = f32[512,640]{1,0:T(8,128)S(1)} custom-call(bf16[640,16384]{1,0:T(8,128)(2,1)} %copy-done, bf16[64,16384]{1,0:T(8,128)(2,1)S(1)} %shard_map.74.refs_0_, bf16[64,16384]{1,0:T(8,128)(2,1)S(1)} %shard_map.75.refs_1_, bf16[64,16384]{1,0:T(8,128)(2,1)S(1)} %shard_map.76.refs_2_, bf16[64,16384]{1,0:T(8,128)(2,1)S(1)} %shard_map.77.refs_3_, ...), custom_call_target="tpu_custom_call" | custom-call | flops 5368709120 | bytes 29360128 | tf_op jit(solution)/shard_map/pallas_call | solution.py:137
  123.1 6.1 %shard_map.73.refs_3_ = bf16[64,16384]{1,0:T(8,128)(2,1)S(1)} custom-call(bf16[8,160,128]{2,1,0:T(8,128)(2,1)S(1)} %collective-permute-done.15.refs_16_.refs_0_, bf16[8,160,128]{2,1,0:T(8,128)(2,1)} %collective-permute-done.16.refs_17_.refs_1_, bf16[8,160,128]{2,1,0:T(8,128)(2,1)S(1)} %collective-permute-done.17.refs_18_.refs_2_, ...), custom_call_target="tpu_custom_call" | custom-call | flops 536870912 | bytes 6291456 | tf_op jit(solution)/shard_map/pallas_call | solution.py:92
  129.2 6.2 %shard_map.72.refs_2_ = bf16[64,16384]{1,0:T(8,128)(2,1)S(1)} custom-call(bf16[16,160,128]{2,1,0:T(8,128)(2,1)} %collective-permute-done.13.refs_14_.refs_0_, bf16[16,160,128]{2,1,0:T(8,128)(2,1)S(1)} %collective-permute-done.14.refs_15_.refs_1_), custom_call_target="tpu_custom_call" | custom-call | flops 536870912 | bytes 6291456 | tf_op jit(solution)/shard_map/pallas_call | solution.py:92
  135.5 4.9 %shard_map.71.refs_1_ = bf16[64,16384]{1,0:T(8,128)(2,1)S(1)} custom-call(bf16[16,160,128]{2,1,0:T(8,128)(2,1)S(1)} %collective-permute-done.11.refs_12_.refs_0_, bf16[16,160,128]{2,1,0:T(8,128)(2,1)S(1)} %collective-permute-done.12.refs_13_.refs_1_), custom_call_target="tpu_custom_call" | custom-call | flops 536870912 | bytes 6291456 | tf_op jit(solution)/shard_map/pallas_call | solution.py:92
  140.4 16.7 %shard_map.79 = bf16[512,640]{1,0:T(8,128)(2,1)S(1)} custom-call(bf16[640,16384]{1,0:T(8,128)(2,1)} %copy-done, bf16[64,16384]{1,0:T(8,128)(2,1)S(1)} %shard_map.70.refs_0_, bf16[64,16384]{1,0:T(8,128)(2,1)S(1)} %shard_map.71.refs_1_, bf16[64,16384]{1,0:T(8,128)(2,1)S(1)} %shard_map.72.refs_2_, bf16[64,16384]{1,0:T(8,128)(2,1)S(1)} %shard_map.73.refs_3_, ...), custom_call_target="tpu_custom_call" | custom-call | flops 5368709120 | bytes 29360128 | tf_op jit(solution)/shard_map/pallas_call | solution.py:137
  159.0 3.0 %collective-permute-start.25 = (bf16[64,640]{1,0:T(8,128)(2,1)S(1)}, bf16[64,640]{1,0:T(8,128)(2,1)S(1)}, u32[]{:S(2)}, u32[]{:S(2)}) collective-permute-start(bf16[64,640]{1,0:T(8,128)(2,1)S(1)} %get-tuple-element.5), channel_id=1, source_target_pairs={{0,112},{16,96},{32,16},{48,0},{64,48},{80,32},{96,80},{112,64},{1... | collective-permute-start | bytes 245768 | tf_op jit(solution)/shard_map/ppermute | solution.py:265
  164.8 3.2 %collective-permute-start.22 = (bf16[64,640]{1,0:T(8,128)(2,1)S(1)}, bf16[64,640]{1,0:T(8,128)(2,1)S(1)}, u32[]{:S(2)}, u32[]{:S(2)}) collective-permute-start(bf16[64,640]{1,0:T(8,128)(2,1)S(1)} %get-tuple-element.8), channel_id=1, source_target_pairs={{0,64},{16,80},{32,96},{48,112},{64,0},{80,16},{96,32},{112,48},{1... | collective-permute-start | bytes 245768 | tf_op jit(solution)/shard_map/ppermute | solution.py:265
  170.0 17.8 %shard_map.68 = bf16[16,128,128]{2,1,0:T(8,128)(2,1)} custom-call(s32[16]{0:T(128)} %copy-done.18, s32[16]{0:T(128)} %and_select_fusion.row_ref, bf16[16,160,128]{2,1,0:T(8,128)(2,1)} %copy-done.1, bf16[16,160,128]{2,1,0:T(8,128)(2,1)} %copy-done.5, bf16[16,160,128]{2,1,0:T(8,128)(2,1)} %copy-done.4, bf16[16,160,128]{2,1,0:T(8,128)(2,1)} %copy-done.7, ...), custom_call_target="tpu_custom_call" | custom-call | tf_op jit(solution)/shard_map/pallas_call | solution.py:173
  (130 shorter events, 25.6 us)
Async XLA Ops:
  3.6 18.2 %collective-permute-start.5 = (bf16[16,160,128]{2,1,0:T(8,128)(2,1)S(1)}, bf16[16,160,128]{2,1,0:T(8,128)(2,1)S(1)}, u32[]{:S(2)}, u32[]{:S(2)}) collective-permute-start(bf16[16,160,128]{2,1,0:T(8,128)(2,1)S(1)} %constant_dynamic-update-slice_fusion.refs_0_), channel_id=1, source_target_pairs={{0,6},{1,7},{2,0},{3,1},{4,2},{5,3},{6,4},{7,5},{8,14},{9,15},{10,... | collective-permute-start | bytes 1966088 | tf_op jit(solution)/shard_map/ppermute | solution.py:203
  7.8 21.5 %collective-permute-start.3 = (bf16[16,160,128]{2,1,0:T(8,128)(2,1)S(1)}, bf16[16,160,128]{2,1,0:T(8,128)(2,1)S(1)}, u32[]{:S(2)}, u32[]{:S(2)}) collective-permute-start(bf16[16,160,128]{2,1,0:T(8,128)(2,1)S(1)} %constant_dynamic-update-slice_fusion.refs_0_), channel_id=1, source_target_pairs={{0,2},{1,3},{2,4},{3,5},{4,6},{5,7},{6,0},{7,1},{8,10},{9,11},{10,... | collective-permute-start | bytes 1966088 | tf_op jit(solution)/shard_map/ppermute | solution.py:203
  7.8 27.5 %collective-permute-start.1 = (bf16[16,160,128]{2,1,0:T(8,128)(2,1)S(1)}, bf16[16,160,128]{2,1,0:T(8,128)(2,1)S(1)}, u32[]{:S(2)}, u32[]{:S(2)}) collective-permute-start(bf16[16,160,128]{2,1,0:T(8,128)(2,1)S(1)} %constant_dynamic-update-slice_fusion.refs_0_), channel_id=1, source_target_pairs={{0,8},{1,9},{2,10},{3,11},{4,12},{5,13},{6,14},{7,15},{8,0},{9,1},... | collective-permute-start | bytes 1966088 | tf_op jit(solution)/shard_map/ppermute | solution.py:203
  10.8 25.0 %collective-permute-start = (bf16[16,160,128]{2,1,0:T(8,128)(2,1)S(1)}, bf16[16,160,128]{2,1,0:T(8,128)(2,1)S(1)}, u32[]{:S(2)}, u32[]{:S(2)}) collective-permute-start(bf16[16,160,128]{2,1,0:T(8,128)(2,1)S(1)} %constant_dynamic-update-slice_fusion.refs_0_), channel_id=1, source_target_pairs={{0,1},{1,0},{2,3},{3,2},{4,5},{5,4},{6,7},{7,6},{8,9},{9,8},{10,11... | collective-permute-start | bytes 1966088 | tf_op jit(solution)/shard_map/ppermute | solution.py:203
  30.1 19.9 %collective-permute-start.7 = (bf16[8,160,128]{2,1,0:T(8,128)(2,1)}, bf16[8,160,128]{2,1,0:T(8,128)(2,1)}, u32[]{:S(2)}, u32[]{:S(2)}) collective-permute-start(bf16[8,160,128]{2,1,0:T(8,128)(2,1)} %slice.44), channel_id=1, source_target_pairs={{0,2},{1,3},{2,4},{3,5},{4,6},{5,7},{6,0},{7,1},{8,10},{9,11},{10,... | collective-permute-start | bytes 983048 | tf_op jit(solution)/shard_map/ppermute | solution.py:203
  31.7 18.5 %collective-permute-start.16 = (bf16[8,160,128]{2,1,0:T(8,128)(2,1)}, bf16[8,160,128]{2,1,0:T(8,128)(2,1)}, u32[]{:S(2)}, u32[]{:S(2)}) collective-permute-start(bf16[8,160,128]{2,1,0:T(8,128)(2,1)} %collective-permute-done.8.refs_9_.refs_1_), channel_id=1, source_target_pairs={{0,8},{1,9},{2,10},{3,11},{4,12},{5,13},{6,14},{7,15},{8,0},{9,1},... | collective-permute-start | bytes 983048 | tf_op jit(solution)/shard_map/ppermute | solution.py:203
  35.3 40.0 %collective-permute-start.6 = (bf16[16,160,128]{2,1,0:T(8,128)(2,1)S(1)}, bf16[16,160,128]{2,1,0:T(8,128)(2,1)}, u32[]{:S(2)}, u32[]{:S(2)}) collective-permute-start(bf16[16,160,128]{2,1,0:T(8,128)(2,1)S(1)} %collective-permute-done.5.refs_6_.refs_0_), channel_id=1, source_target_pairs={{0,1},{1,0},{2,3},{3,2},{4,5},{5,4},{6,7},{7,6},{8,9},{9,8},{10,11... | collective-permute-start | bytes 1966088 | tf_op jit(solution)/shard_map/ppermute | solution.py:203
  35.3 40.5 %collective-permute-start.4 = (bf16[16,160,128]{2,1,0:T(8,128)(2,1)S(1)}, bf16[16,160,128]{2,1,0:T(8,128)(2,1)}, u32[]{:S(2)}, u32[]{:S(2)}) collective-permute-start(bf16[16,160,128]{2,1,0:T(8,128)(2,1)S(1)} %collective-permute-done.3.refs_4_.refs_0_), channel_id=1, source_target_pairs={{0,1},{1,0},{2,3},{3,2},{4,5},{5,4},{6,7},{7,6},{8,9},{9,8},{10,11... | collective-permute-start | bytes 1966088 | tf_op jit(solution)/shard_map/ppermute | solution.py:203
  35.8 40.5 %collective-permute-start.13 = (bf16[16,160,128]{2,1,0:T(8,128)(2,1)S(1)}, bf16[16,160,128]{2,1,0:T(8,128)(2,1)}, u32[]{:S(2)}, u32[]{:S(2)}) collective-permute-start(bf16[16,160,128]{2,1,0:T(8,128)(2,1)S(1)} %collective-permute-done.1.refs_2_.refs_0_), channel_id=1, source_target_pairs={{0,6},{1,7},{2,0},{3,1},{4,2},{5,3},{6,4},{7,5},{8,14},{9,15},{10,... | collective-permute-start | bytes 1966088 | tf_op jit(solution)/shard_map/ppermute | solution.py:203
  50.1 37.2 %collective-permute-start.11 = (bf16[16,160,128]{2,1,0:T(8,128)(2,1)S(1)}, bf16[16,160,128]{2,1,0:T(8,128)(2,1)S(1)}, u32[]{:S(2)}, u32[]{:S(2)}) collective-permute-start(bf16[16,160,128]{2,1,0:T(8,128)(2,1)S(1)} %collective-permute-done.1.refs_2_.refs_0_), channel_id=1, source_target_pairs={{0,2},{1,3},{2,4},{3,5},{4,6},{5,7},{6,0},{7,1},{8,10},{9,11},{10,... | collective-permute-start | bytes 1966088 | tf_op jit(solution)/shard_map/ppermute | solution.py:203
  50.2 43.7 %collective-permute-start.2 = (bf16[16,160,128]{2,1,0:T(8,128)(2,1)S(1)}, bf16[16,160,128]{2,1,0:T(8,128)(2,1)S(1)}, u32[]{:S(2)}, u32[]{:S(2)}) collective-permute-start(bf16[16,160,128]{2,1,0:T(8,128)(2,1)S(1)} %collective-permute-done.1.refs_2_.refs_0_), channel_id=1, source_target_pairs={{0,1},{1,0},{2,3},{3,2},{4,5},{5,4},{6,7},{7,6},{8,9},{9,8},{10,11... | collective-permute-start | bytes 1966088 | tf_op jit(solution)/shard_map/ppermute | solution.py:203
  75.3 23.7 %collective-permute-start.10 = (bf16[8,160,128]{2,1,0:T(8,128)(2,1)}, bf16[8,160,128]{2,1,0:T(8,128)(2,1)S(1)}, u32[]{:S(2)}, u32[]{:S(2)}) collective-permute-start(bf16[8,160,128]{2,1,0:T(8,128)(2,1)} %collective-permute-done.8.refs_9_.refs_1_), channel_id=1, source_target_pairs={{0,1},{1,0},{2,3},{3,2},{4,5},{5,4},{6,7},{7,6},{8,9},{9,8},{10,11... | collective-permute-start | bytes 983048 | tf_op jit(solution)/shard_map/ppermute | solution.py:203
  75.8 23.7 %collective-permute-start.15 = (bf16[8,160,128]{2,1,0:T(8,128)(2,1)}, bf16[8,160,128]{2,1,0:T(8,128)(2,1)S(1)}, u32[]{:S(2)}, u32[]{:S(2)}) collective-permute-start(bf16[8,160,128]{2,1,0:T(8,128)(2,1)} %collective-permute-done.7.refs_8_.refs_0_), channel_id=1, source_target_pairs={{0,8},{1,9},{2,10},{3,11},{4,12},{5,13},{6,14},{7,15},{8,0},{9,1},... | collective-permute-start | bytes 983048 | tf_op jit(solution)/shard_map/ppermute | solution.py:203
  76.3 23.3 %collective-permute-start.9 = (bf16[8,160,128]{2,1,0:T(8,128)(2,1)}, bf16[8,160,128]{2,1,0:T(8,128)(2,1)S(1)}, u32[]{:S(2)}, u32[]{:S(2)}) collective-permute-start(bf16[8,160,128]{2,1,0:T(8,128)(2,1)} %collective-permute-done.7.refs_8_.refs_0_), channel_id=1, source_target_pairs={{0,1},{1,0},{2,3},{3,2},{4,5},{5,4},{6,7},{7,6},{8,9},{9,8},{10,11... | collective-permute-start | bytes 983048 | tf_op jit(solution)/shard_map/ppermute | solution.py:203
  87.3 41.9 %collective-permute-start.14 = (bf16[16,160,128]{2,1,0:T(8,128)(2,1)}, bf16[16,160,128]{2,1,0:T(8,128)(2,1)S(1)}, u32[]{:S(2)}, u32[]{:S(2)}) collective-permute-start(bf16[16,160,128]{2,1,0:T(8,128)(2,1)} %collective-permute-done.13.refs_14_.refs_0_), channel_id=1, source_target_pairs={{0,1},{1,0},{2,3},{3,2},{4,5},{5,4},{6,7},{7,6},{8,9},{9,8},{10,11... | collective-permute-start | bytes 1966088 | tf_op jit(solution)/shard_map/ppermute | solution.py:203
  93.9 41.6 %collective-permute-start.12 = (bf16[16,160,128]{2,1,0:T(8,128)(2,1)S(1)}, bf16[16,160,128]{2,1,0:T(8,128)(2,1)S(1)}, u32[]{:S(2)}, u32[]{:S(2)}) collective-permute-start(bf16[16,160,128]{2,1,0:T(8,128)(2,1)S(1)} %collective-permute-done.11.refs_12_.refs_0_), channel_id=1, source_target_pairs={{0,1},{1,0},{2,3},{3,2},{4,5},{5,4},{6,7},{7,6},{8,9},{9,8},{10,11... | collective-permute-start | bytes 1966088 | tf_op jit(solution)/shard_map/ppermute | solution.py:203
  99.0 24.0 %collective-permute-start.18 = (bf16[8,160,128]{2,1,0:T(8,128)(2,1)}, bf16[8,160,128]{2,1,0:T(8,128)(2,1)S(1)}, u32[]{:S(2)}, u32[]{:S(2)}) collective-permute-start(bf16[8,160,128]{2,1,0:T(8,128)(2,1)} %collective-permute-done.16.refs_17_.refs_1_), channel_id=1, source_target_pairs={{0,1},{1,0},{2,3},{3,2},{4,5},{5,4},{6,7},{7,6},{8,9},{9,8},{10,11... | collective-permute-start | bytes 983048 | tf_op jit(solution)/shard_map/ppermute | solution.py:203
  99.5 23.6 %collective-permute-start.17 = (bf16[8,160,128]{2,1,0:T(8,128)(2,1)S(1)}, bf16[8,160,128]{2,1,0:T(8,128)(2,1)S(1)}, u32[]{:S(2)}, u32[]{:S(2)}) collective-permute-start(bf16[8,160,128]{2,1,0:T(8,128)(2,1)S(1)} %collective-permute-done.15.refs_16_.refs_0_), channel_id=1, source_target_pairs={{0,1},{1,0},{2,3},{3,2},{4,5},{5,4},{6,7},{7,6},{8,9},{9,8},{10,11... | collective-permute-start | bytes 983048 | tf_op jit(solution)/shard_map/ppermute | solution.py:203
  157.2 10.7 %collective-permute-start.19 = (bf16[64,640]{1,0:T(8,128)(2,1)S(1)}, bf16[64,640]{1,0:T(8,128)(2,1)S(1)}, u32[]{:S(2)}, u32[]{:S(2)}) collective-permute-start(bf16[64,640]{1,0:T(8,128)(2,1)S(1)} %get-tuple-element.4), channel_id=1, source_target_pairs={{0,16},{16,0},{32,48},{48,32},{64,80},{80,64},{96,112},{112,96},{1... | collective-permute-start | bytes 245768 | tf_op jit(solution)/shard_map/ppermute | solution.py:265
  162.7 25.2 %collective-permute-start.24 = (bf16[64,640]{1,0:T(8,128)(2,1)S(1)}, bf16[64,640]{1,0:T(8,128)(2,1)S(1)}, u32[]{:S(2)}, u32[]{:S(2)}) collective-permute-start(bf16[64,640]{1,0:T(8,128)(2,1)S(1)} %get-tuple-element.6), channel_id=1, source_target_pairs={{0,96},{16,112},{32,0},{48,16},{64,32},{80,48},{96,64},{112,80},{1... | collective-permute-start | bytes 245768 | tf_op jit(solution)/shard_map/ppermute | solution.py:265
  163.5 24.4 %collective-permute-start.23 = (bf16[64,640]{1,0:T(8,128)(2,1)S(1)}, bf16[64,640]{1,0:T(8,128)(2,1)S(1)}, u32[]{:S(2)}, u32[]{:S(2)}) collective-permute-start(bf16[64,640]{1,0:T(8,128)(2,1)S(1)} %get-tuple-element.7), channel_id=1, source_target_pairs={{0,80},{16,64},{32,112},{48,96},{64,16},{80,0},{96,48},{112,32},{1... | collective-permute-start | bytes 245768 | tf_op jit(solution)/shard_map/ppermute | solution.py:265
  164.8 23.1 %collective-permute-start.22 = (bf16[64,640]{1,0:T(8,128)(2,1)S(1)}, bf16[64,640]{1,0:T(8,128)(2,1)S(1)}, u32[]{:S(2)}, u32[]{:S(2)}) collective-permute-start(bf16[64,640]{1,0:T(8,128)(2,1)S(1)} %get-tuple-element.8), channel_id=1, source_target_pairs={{0,64},{16,80},{32,96},{48,112},{64,0},{80,16},{96,32},{112,48},{1... | collective-permute-start | bytes 245768 | tf_op jit(solution)/shard_map/ppermute | solution.py:265
  168.0 19.9 %collective-permute-start.21 = (bf16[64,640]{1,0:T(8,128)(2,1)S(1)}, bf16[64,640]{1,0:T(8,128)(2,1)S(1)}, u32[]{:S(2)}, u32[]{:S(2)}) collective-permute-start(bf16[64,640]{1,0:T(8,128)(2,1)S(1)} %get-tuple-element.9), channel_id=1, source_target_pairs={{0,48},{16,32},{32,80},{48,64},{64,112},{80,96},{96,16},{112,0},{1... | collective-permute-start | bytes 245768 | tf_op jit(solution)/shard_map/ppermute | solution.py:265
  169.2 18.7 %collective-permute-start.20 = (bf16[64,640]{1,0:T(8,128)(2,1)S(1)}, bf16[64,640]{1,0:T(8,128)(2,1)S(1)}, u32[]{:S(2)}, u32[]{:S(2)}) collective-permute-start(bf16[64,640]{1,0:T(8,128)(2,1)S(1)} %get-tuple-element.10), channel_id=1, source_target_pairs={{0,32},{16,48},{32,64},{48,80},{64,96},{80,112},{96,0},{112,16},{1... | collective-permute-start | bytes 245768 | tf_op jit(solution)/shard_map/ppermute | solution.py:265
  (21 other events, 549.8 us)

commit v2 on v0

v2 whole, which is shorter than its diff:
```python
import functools

import jax
import jax.numpy as jnp
from jax import lax
from jax.experimental import pallas as pl
from jax.experimental.pallas import tpu as pltpu
from jax.sharding import PartitionSpec as P

BF = jnp.bfloat16
F32 = jnp.float32
WHOLE = pl.BlockSpec(memory_space=pltpu.VMEM)


def near(value):
    return pltpu.with_memory_space_constraint(value, pltpu.VMEM)


def swap_matrix():
    row = lax.broadcasted_iota(jnp.int32, (256, 256), 0)
    col = lax.broadcasted_iota(jnp.int32, (256, 256), 1)
    hit = (row // 16 == col % 16) & (row % 16 == col // 16)
    return jnp.where(hit, 1.0, 0.0).astype(BF)


def flatten_kernel(start, v_ref, out_ref, held, came):
    count = held.shape[0]
    loads = [
        pltpu.make_async_copy(
            v_ref.at[pl.ds(start + g, 32)], held.at[pl.ds(g, 32)], came.at[g // 32]
        )
        for g in range(0, count, 32)
    ]
    for load in loads:
        load.start()
    swap = swap_matrix()
    for n, load in enumerate(loads):
        load.wait()
        for p in range(0, 128, 16):
            pair = [
                held[n * 32 + g : n * 32 + g + 16, p : p + 16, :].reshape(256, 128)
                for g in (0, 16)
            ]
            both = jnp.dot(
                swap, jnp.concatenate(pair, axis=1), preferred_element_type=F32
            ).astype(BF)
            for q in range(16):
                for h in range(2):
                    row = n * 32 + h * 16
                    out_ref[row : row + 16, (p + q) * 128 : (p + q + 1) * 128] = both[
                        q * 16 : q * 16 + 16, h * 128 : h * 128 + 128
                    ]


def flatten_vectors(vectors, start, count):
    return pl.pallas_call(
        functools.partial(flatten_kernel, start),
        in_specs=[pl.BlockSpec(memory_space=pl.ANY)],
        out_specs=WHOLE,
        out_shape=pltpu.VMEM((count, 16384), BF),
        scratch_shapes=[
            pltpu.VMEM((count, 128, 128), BF),
            pltpu.SemaphoreType.DMA((count // 32,)),
        ],
        compiler_params=pltpu.CompilerParams(vmem_limit_bytes=10 << 20),
        cost_estimate=pl.CostEstimate(
            flops=2 * count * 16384 * 256, bytes_accessed=4 * count * 16384, transcendentals=0
        ),
    )(pltpu.with_memory_space_constraint(vectors, pltpu.HBM))


def pack_kernel(walk_ref, inv_ref, out_ref):
    out_ref[:, 0:128, :] = walk_ref[...]
    for w in range(16):
        blocks = [inv_ref[w, 32 * n : 32 * n + 32, :] for n in range(4)]
        out_ref[w, 128:160, :] = jnp.concatenate(blocks, axis=1)


def pack(walkers, inverse):
    return pl.pallas_call(
        pack_kernel,
        in_specs=[WHOLE] * 2,
        out_specs=WHOLE,
        out_shape=pltpu.VMEM((16, 160, 128), BF),
        compiler_params=pltpu.CompilerParams(vmem_limit_bytes=6 << 20),
        cost_estimate=pl.CostEstimate(flops=0, bytes_accessed=2 << 20, transcendentals=0),
    )(walkers, inverse.reshape(16, 128, 32))


def theta_kernel(*refs):
    refs, out_ref, work = refs[:-2], refs[-2], refs[-1]
    swap = swap_matrix()
    lane = lax.broadcasted_iota(jnp.int32, (32, 128), 1)
    sign = jnp.where(lane < 64, 1.0, -1.0)
    keep0 = jnp.where(lane % 64 < 32, 1.0, 0.0)
    keep1 = 1.0 - keep0
    size = 16 // len(refs)
    for w in range(16):
        ref = refs[w // size]
        small = ref[w % size, 128:160, :].astype(F32)
        a = small * sign
        b = -jnp.concatenate([small[:, 64:], small[:, :64]], axis=1)
        operator = jnp.concatenate([a * keep0, a * keep1, b * keep0, b * keep1], axis=0).astype(BF)
        work[w] = jnp.dot(
            ref[w % size, 0:128, :], operator, preferred_element_type=F32
        ).astype(BF)
    for p in range(0, 128, 32):
        pair = [work[:, q : q + 16, :].reshape(256, 128) for q in (p, p + 16)]
        both = jnp.dot(
            swap, jnp.concatenate(pair, axis=1), preferred_element_type=F32
        ).astype(BF)
        for h in range(2):
            for q in range(16):
                at = (p + h * 16 + q) * 128
                out_ref[:, at : at + 128] = both[q * 16 : q * 16 + 16, h * 128 : h * 128 + 128]


def theta_of(*pieces):
    return pl.pallas_call(
        theta_kernel,
        in_specs=[WHOLE] * len(pieces),
        out_specs=WHOLE,
        out_shape=pltpu.VMEM((16, 16384), BF),
        scratch_shapes=[pltpu.VMEM((16, 128, 128), BF)],
        compiler_params=pltpu.CompilerParams(vmem_limit_bytes=6 << 20),
        cost_estimate=pl.CostEstimate(
            flops=2 * 16 * 16384 * 256, bytes_accessed=2 << 20, transcendentals=0
        ),
    )(*[near(piece) for piece in pieces])


OFFSETS = ((0, 0), (1, 0), (0, -1), (0, 1), (0, 2), (1, -1), (1, 1), (1, 2))


def place():
    me = lax.axis_index("walk")
    return me >> 3, me >> 1 & 3, me & 1


def product_kernel(part, *refs):
    flats, thetas, source_ref = refs[:4], refs[4:12], refs[12]
    rest = refs[13:]
    acc = rest[-1]
    depth = 4096
    for start in range(0, 16384, depth):
        span = slice(start, start + depth)
        first = jnp.concatenate([t[:, span] for t in thetas], axis=0)
        turned = []
        for n in range(0, depth, 128):
            turned += [-first[:, n + 64 : n + 128], first[:, n : n + 64]]
        both = jnp.concatenate([first, jnp.concatenate(turned, axis=1)], axis=0)
        flat = jnp.concatenate([f[:, span] for f in flats], axis=0)
        product = lax.dot_general(
            flat, both, (((1,), (1,)), ((), ())), preferred_element_type=F32
        )
        if start == 0:
            acc[...] = product
        else:
            acc[...] += product
    bias = acc[...].astype(BF)

    vec = lax.axis_index("vec")
    row = lax.broadcasted_iota(jnp.int32, (256, 256), 0)
    col = lax.broadcasted_iota(jnp.int32, (256, 256), 1)
    target = (((vec >> 1) + (row >> 6)) & 3) * 2 + ((vec + (row >> 5)) & 1)
    sources = jnp.concatenate([source_ref[0:1, :], source_ref[1:2, :]], axis=1)
    found = jnp.where(col == target * 32 + (row & 31), jnp.broadcast_to(sources, (256, 256)), 0)
    wanted = jnp.sum(found, axis=1, keepdims=True)
    x, z, core = place()
    slot = lax.broadcasted_iota(jnp.int32, (256, 128), 1)
    dx, dz = jnp.zeros_like(slot), jnp.zeros_like(slot)
    for n, (sx, sz) in enumerate(OFFSETS[part * 4 : part * 4 + 4]):
        here = (slot >> 4 & 3) == n
        dx = jnp.where(here, sx, dx)
        dz = jnp.where(here, sz, dz)
    old = ((x ^ dx) * 4 + (z + dz & 3)) * 32 + ((core ^ (slot >> 6)) * 16 + (slot & 15))
    pick = jnp.where(wanted == old, 1.0, 0.0).astype(BF)
    for c in range(2):
        picked = lax.dot_general(
            pick,
            bias[:, c * 128 : c * 128 + 128],
            (((1,), (1,)), ((), ())),
            preferred_element_type=F32,
        )
        if part == 0:
            rest[0][c] = picked
        else:
            picked = picked + rest[0][c]
            rest[1][c] = picked[0:32]
            for n in range(1, 8):
                rest[n + 1][c] = picked[n * 32 : n * 32 + 32].astype(BF)


def product(part, flats, thetas, sources, before):
    count = sum(f.shape[0] for f in flats)
    if part:
        shapes = [pltpu.VMEM((2, 32, count), F32)] + [pltpu.VMEM((2, 32, count), BF)] * 7
    else:
        shapes = [pltpu.VMEM((2, 256, count), F32)]
    operands = [near(a) for a in [*flats, *thetas, sources, *before]]
    return pl.pallas_call(
        functools.partial(product_kernel, part),
        in_specs=[WHOLE] * len(operands),
        out_specs=[WHOLE] * len(shapes),
        out_shape=shapes,
        scratch_shapes=[pltpu.VMEM((count, 256), F32)],
        compiler_params=pltpu.CompilerParams(vmem_limit_bytes=14 << 20),
        cost_estimate=pl.CostEstimate(
            flops=2 * count * 16384 * 256, bytes_accessed=2 * (count + 256) * 16384, transcendentals=0
        ),
    )(*operands)


def choose_kernel(source_ref, *refs):
    pieces, outs, table, came, went = refs[:-5], refs[-5:-3], refs[-3], refs[-2], refs[-1]
    loads, base = [], 0
    for n, src in enumerate(pieces):
        size = src.shape[0]
        loads.append(
            pltpu.make_async_copy(
                src.at[:, pl.ds(0, 128), :], table.at[pl.ds(base, size)], came.at[n]
            )
        )
        base += size
    for load in loads:
        load.start()
    x, z, core = place()
    me = lax.axis_index("walk")
    slots = []
    for j in range(32):
        source = source_ref[(me ^ (j // 16)) * 16 + j % 16]
        dx, dz = x ^ (source >> 7), ((source >> 5) - z) & 3
        piece = jnp.int32(0)
        for n, (sx, sz) in enumerate(OFFSETS):
            piece = jnp.where((dx == sx) & (dz == sz % 4), n, piece)
        slots.append(piece * 16 + (source & 15))
    for load in loads:
        load.wait()
    stores = [
        pltpu.make_async_copy(table.at[slots[j]], outs[j // 16].at[j % 16], went.at[j])
        for j in range(32)
    ]
    for store in stores:
        store.start()
    for store in stores:
        store.wait()


def choose(sources, pieces):
    shape = pltpu.VMEM((16, 128, 128), BF)
    return pl.pallas_call(
        choose_kernel,
        in_specs=[pl.BlockSpec(memory_space=pltpu.SMEM)] + [WHOLE] * len(pieces),
        out_specs=[WHOLE] * 2,
        scratch_shapes=[
            pltpu.VMEM((128, 128, 128), BF),
            pltpu.SemaphoreType.DMA((len(pieces),)),
            pltpu.SemaphoreType.DMA((32,)),
        ],
        out_shape=[shape, shape],
        compiler_params=pltpu.CompilerParams(vmem_limit_bytes=8 << 20),
        cost_estimate=pl.CostEstimate(flops=0, bytes_accessed=6 << 20, transcendentals=0),
    )(sources, *[near(piece) for piece in pieces])


def finish_kernel(source_ref, mine_ref, theirs_ref, *refs):
    sums, moved_ref, total_ref = refs[:-2], refs[-2], refs[-1]
    me = lax.axis_index("walk")
    for j in range(16):
        here = (source_ref[me * 16 + j] >> 4 & 1) == (me & 1)
        moved_ref[j] = jnp.where(here, mine_ref[j], theirs_ref[j])
    total = sums[0][...]
    for part in sums[1:]:
        total = total + part[...].astype(F32)
    total_ref[...] = total


def finish(sources, mine, theirs, sums):
    operands = [near(a) for a in [mine, theirs, *sums]]
    return pl.pallas_call(
        finish_kernel,
        in_specs=[pl.BlockSpec(memory_space=pltpu.SMEM)] + [WHOLE] * len(operands),
        out_specs=[WHOLE] * 2,
        out_shape=[
            jax.ShapeDtypeStruct(mine.shape, BF),
            jax.ShapeDtypeStruct(sums[0].shape, F32),
        ],
        compiler_params=pltpu.CompilerParams(vmem_limit_bytes=8 << 20),
        cost_estimate=pl.CostEstimate(flops=0, bytes_accessed=3 << 20, transcendentals=0),
    )(sources, *operands)


def index(x, z, core):
    return (x % 2 * 4 + z % 4) * 2 + core


def moves(step):
    return [
        (index(x, z, c), index(*step(x, z, c))) for x in range(2) for z in range(4) for c in range(2)
    ]


ACROSS = moves(lambda x, z, c: (x + 1, z, c))
UP = moves(lambda x, z, c: (x, z + 1, c))
DOWN = moves(lambda x, z, c: (x, z - 1, c))
OTHER = moves(lambda x, z, c: (x, z, 1 - c))


def send(value, pairs):
    return lax.ppermute(value, "walk", pairs)


def after(values, work):
    return lax.optimization_barrier((values, work))


def per_device(walkers, inverse, vectors, sources):
    own = pack(walkers, inverse)
    first = [send(own, pairs) for pairs in (UP, DOWN, ACROSS)]
    flats = [flatten_vectors(vectors, n * 160, 160) for n in range(4)]
    thetas = [theta_of(own)]
    first, (flats[:3], thetas) = after(first, (flats[:3], thetas))
    below, above, across = first
    far = [send(below[:8], UP), send(above[8:], DOWN)]
    across_below = send(across, UP)
    across_above = send(across, DOWN)
    thetas += [theta_of(piece) for piece in (across, below, above)]
    far, (flats[3], thetas) = after(far, (flats[3], thetas))
    across_far = [send(part, ACROSS) for part in far]
    thetas.append(theta_of(*far))
    thetas = [(t, send(t, OTHER)) for t in thetas]
    short = sources.reshape(2, 128)
    operands = [t[0] for t in thetas[:4]] + [t[1] for t in thetas[:4]]
    sums = product(0, flats, operands, short, [])
    second = [across_below, across_above, across_far]
    second, sums = after(second, sums)
    across_below, across_above, across_far = second
    more = [theta_of(across_below), theta_of(across_above), theta_of(*across_far)]
    thetas += [(t, send(t, OTHER)) for t in more]
    operands = [t[0] for t in thetas[4:]] + [t[1] for t in thetas[4:]]
    pieces = [own, across, below, above, *far, across_below, across_above, *across_far]
    mine, theirs = choose(sources, pieces)
    sums = list(product(1, flats, operands, short, sums))

    for k in range(1, 8):
        pairs = [
            (y * 2 + v, ((y + k // 2) % 4) * 2 + (v + k) % 2) for y in range(4) for v in range(2)
        ]
        sums[k] = lax.ppermute(sums[k], "vec", pairs)
    return tuple(finish(sources, mine, send(theirs, OTHER), sums))


def solution(mesh):
    in_specs = (
        P("walk", "vec", None),
        P("walk", None, None, None, None),
        P("walk", "vec", None),
        P(),
    )
    out_specs = (P("walk", "vec", None), P(None, "vec", "walk"))
    return jax.shard_map(
        per_device, mesh=mesh, in_specs=in_specs, out_specs=out_specs, check_vma=False
    )
```

time: 383 us -> 88.1 us (0.23)
  waiting for transfers between devices: 218 us -> 19.6 us
  local copies, waits for them, and re-layouts: 108 us -> 2.13 us
  Pallas kernels: 0 us -> 36.4 us
  matrix products: 29.3 us -> 0 us
  starting transfers between devices: 0.34 us -> 29 us
  between operations: 13.8 us -> 0.83 us
  other arithmetic: 11.2 us -> 0 us
    all_gather x3 -> x0, waiting for transfers between devices: 178 us -> none  [the longest x1 76.6 us: per_device(): piece_inverse = lax.all_gather(inverse, 'walk', axis=0, tiled=True)]
    another operation x5 -> x0, local copies, waits for them, and re-layouts: 52.3 us -> none  [the longest x2 23.7 us: rows_of(): return jnp.stack([first, second], 0)]
    reduce_scatter x1 -> x0, waiting for transfers between devices: 38.7 us -> none  [per_device(): lax.psum_scatter(partial_bias, 'vec', scatter_dimension=1, tiled=True)]
    pallas_call x0 -> x17, Pallas kernels: none -> 36.4 us  [the longest x4 13.9 us: flatten_vectors(): pl.pallas_call(functools.partial(flatten_kernel, start), in_specs=[pl.Blo...]
    reshape x2 -> x0, local copies, waits for them, and re-layouts: 31.8 us -> none  [the longest x1 31.4 us: per_device(): flat_vectors = vectors.reshape(vectors.shape[0], -1)]
    dot_general x4 -> x0, matrix products: 29.3 us -> none  [the longest x1 18.9 us: bias_terms(): lax.dot_general(stacked, flat_vectors, (((1,), (1,)), ((), ())), preferre...]
    ppermute x0 -> x25, starting transfers between devices: none -> 29 us  [the longest x18 16.8 us: send(): return lax.ppermute(value, 'walk', pairs)]
    all_gather x2 -> x0, local copies, waits for them, and re-layouts: 21 us -> none  [the longest x1 11.9 us: per_device(): lax.all_gather(theta, 'walk', axis=0, tiled=True)]
  transfers between devices with their start and end apart: 4 -> 25, of which waited for: 4 -> 10; matrix products, arithmetic and copies ran while one was open for 12% -> 0% of each run, Pallas kernels for 0% -> 39%
where the time goes in v2:
time: 88.1 us; the launch traced here: 87.9 us
  Pallas kernels  36.4 us (41%)
  starting transfers between devices  29 us (33%)
  waiting for transfers between devices  19.6 us (22%)
  local copies, waits for them, and re-layouts  2.13 us (2%)
    ppermute x18, starting transfers between devices, send(): return lax.ppermute(value, 'walk', pairs)  16.8 us
    ppermute x18, waiting for transfers between devices, send(): return lax.ppermute(value, 'walk', pairs)  16.4 us
    pallas_call x4, Pallas kernels, flatten_vectors(): pl.pallas_call(functools.partial(flatten_kernel, start), in_specs=[pl.Blo...  13.9 us
    pallas_call x2, Pallas kernels, product(): pl.pallas_call(functools.partial(product_kernel, part), in_specs=[WHOLE]...  12.3 us
    ppermute x7, starting transfers between devices, per_device(): sums[k] = lax.ppermute(sums[k], 'vec', pairs)  12.2 us
    pallas_call x8, Pallas kernels, theta_of(): pl.pallas_call(theta_kernel, in_specs=[WHOLE] * len(pieces), out_specs=WH...  5.3 us
    ppermute x7, waiting for transfers between devices, per_device(): sums[k] = lax.ppermute(sums[k], 'vec', pairs)  3.13 us
    pallas_call x1, Pallas kernels, choose(): pl.pallas_call(choose_kernel, in_specs=[pl.BlockSpec(memory_space=pltpu.S...  3.11 us
  transfers between devices with their start and end apart: 25, of which 10 were waited for; matrix products, arithmetic and copies ran while one was open for 0% of the time, Pallas kernels for 39%

profile of v2, /device:TPU:0, one launch (start us, length us, event | category | flops | bytes accessed | tf_op | source)
XLA Modules:
  0.0 87.9 jit_solution(8929275196114424250)
XLA Ops:
  2.9 3.2 %collective-permute-start.2 = (bf16[16,160,128]{2,1,0:T(8,128)(2,1)S(1)}, bf16[16,160,128]{2,1,0:T(8,128)(2,1)S(1)}, u32[]{:S(2)}, u32[]{:S(2)}) collective-permute-start(bf16[16,160,128]{2,1,0:T(8,128)(2,1)S(1)} %shard_map.59.refs_0_), channel_id=1, source_target_pairs={{0,8},{1,9},{2,10},{3,11},{4,12},{5,13},{6,14},{7,15},{8,0},{9,1},... | collective-permute-start | bytes 1966088 | tf_op jit(solution)/shard_map/ppermute | solution.py:310
  6.1 4.0 %collective-permute-start.1 = (bf16[16,160,128]{2,1,0:T(8,128)(2,1)S(1)}, bf16[16,160,128]{2,1,0:T(8,128)(2,1)S(1)}, u32[]{:S(2)}, u32[]{:S(2)}) collective-permute-start(bf16[16,160,128]{2,1,0:T(8,128)(2,1)S(1)} %shard_map.59.refs_0_), channel_id=1, source_target_pairs={{0,6},{1,7},{2,0},{3,1},{4,2},{5,3},{6,4},{7,5},{8,14},{9,15},{10,... | collective-permute-start | bytes 1966088 | tf_op jit(solution)/shard_map/ppermute | solution.py:310
  10.8 3.5 %shard_map.61.refs_1_ = bf16[160,16384]{1,0:T(8,128)(2,1)S(1)} custom-call(bf16[640,128,128]{2,1,0:T(8,128)(2,1)} %v_ref.7), custom_call_target="tpu_custom_call" | custom-call | flops 1342177280 | bytes 10485760 | tf_op jit(solution)/shard_map/pallas_call | solution.py:56
  14.3 3.5 %shard_map.60.refs_0_ = bf16[160,16384]{1,0:T(8,128)(2,1)S(1)} custom-call(bf16[640,128,128]{2,1,0:T(8,128)(2,1)} %v_ref.7), custom_call_target="tpu_custom_call" | custom-call | flops 1342177280 | bytes 10485760 | tf_op jit(solution)/shard_map/pallas_call | solution.py:56
  17.8 3.5 %shard_map.62.refs_2_ = bf16[160,16384]{1,0:T(8,128)(2,1)S(1)} custom-call(bf16[640,128,128]{2,1,0:T(8,128)(2,1)} %v_ref.7), custom_call_target="tpu_custom_call" | custom-call | flops 1342177280 | bytes 10485760 | tf_op jit(solution)/shard_map/pallas_call | solution.py:56
  21.3 2.6 %collective-permute-done.1.refs_0_.refs_3_ = bf16[16,160,128]{2,1,0:T(8,128)(2,1)S(1)} collective-permute-done((bf16[16,160,128]{2,1,0:T(8,128)(2,1)S(1)}, bf16[16,160,128]{2,1,0:T(8,128)(2,1)S(1)}, u32[]{:S(2)}, u32[]{:S(2)}) %collective-permute-start.1) | collective-permute-done | bytes 655392 | tf_op jit(solution)/shard_map/ppermute | solution.py:310
  23.8 3.4 %collective-permute-done.refs_0_.refs_2_ = bf16[16,160,128]{2,1,0:T(8,128)(2,1)S(1)} collective-permute-done((bf16[16,160,128]{2,1,0:T(8,128)(2,1)S(1)}, bf16[16,160,128]{2,1,0:T(8,128)(2,1)S(1)}, u32[]{:S(2)}, u32[]{:S(2)}) %collective-permute-start) | collective-permute-done | bytes 655392 | tf_op jit(solution)/shard_map/ppermute | solution.py:310
  27.7 1.7 %collective-permute-start.3 = (bf16[8,160,128]{2,1,0:T(8,128)(2,1)S(1)}, bf16[8,160,128]{2,1,0:T(8,128)(2,1)S(1)}, u32[]{:S(2)}, u32[]{:S(2)}) collective-permute-start(bf16[8,160,128]{2,1,0:T(8,128)(2,1)S(1)} %slice.6), channel_id=1, source_target_pairs={{0,2},{1,3},{2,4},{3,5},{4,6},{5,7},{6,0},{7,1},{8,10},{9,11},{10,... | collective-permute-start | bytes 983048 | tf_op jit(solution)/shard_map/ppermute | solution.py:310
  29.4 3.5 %shard_map.64.refs_3_ = bf16[160,16384]{1,0:T(8,128)(2,1)S(1)} custom-call(bf16[640,128,128]{2,1,0:T(8,128)(2,1)} %v_ref.7), custom_call_target="tpu_custom_call" | custom-call | flops 1342177280 | bytes 10485760 | tf_op jit(solution)/shard_map/pallas_call | solution.py:56
  35.3 1.5 %collective-permute-done.3.refs_4_.refs_0_ = bf16[8,160,128]{2,1,0:T(8,128)(2,1)S(1)} collective-permute-done((bf16[8,160,128]{2,1,0:T(8,128)(2,1)S(1)}, bf16[8,160,128]{2,1,0:T(8,128)(2,1)S(1)}, u32[]{:S(2)}, u32[]{:S(2)}) %collective-permute-start.3) | collective-permute-done | bytes 327712 | tf_op jit(solution)/shard_map/ppermute | solution.py:310
  41.6 2.6 %collective-permute-start.8 = (bf16[8,160,128]{2,1,0:T(8,128)(2,1)S(1)}, bf16[8,160,128]{2,1,0:T(8,128)(2,1)S(1)}, u32[]{:S(2)}, u32[]{:S(2)}) collective-permute-start(bf16[8,160,128]{2,1,0:T(8,128)(2,1)S(1)} %collective-permute-done.4.refs_5_.refs_1_), channel_id=1, source_target_pairs={{0,8},{1,9},{2,10},{3,11},{4,12},{5,13},{6,14},{7,15},{8,0},{9,1},... | collective-permute-start | bytes 983048 | tf_op jit(solution)/shard_map/ppermute | solution.py:310
  44.2 6.2 %shard_map.68.refs_13_ = f32[2,256,640]{2,1,0:T(8,128)S(1)} custom-call(bf16[160,16384]{1,0:T(8,128)(2,1)S(1)} %shard_map.60.refs_0_, bf16[160,16384]{1,0:T(8,128)(2,1)S(1)} %shard_map.61.refs_1_, bf16[160,16384]{1,0:T(8,128)(2,1)S(1)} %shard_map.62.refs_2_, bf16[160,16384]{1,0:T(8,128)(2,1)S(1)} %shard_map.64.refs_3_, ...), custom_call_target="tpu_custom_call" | custom-call | flops 5368709120 | bytes 29360128 | tf_op jit(solution)/shard_map/pallas_call | solution.py:201
  50.4 2.4 %collective-permute-done.7.refs_8_.refs_0_ = bf16[8,160,128]{2,1,0:T(8,128)(2,1)S(1)} collective-permute-done((bf16[8,160,128]{2,1,0:T(8,128)(2,1)S(1)}, bf16[8,160,128]{2,1,0:T(8,128)(2,1)S(1)}, u32[]{:S(2)}, u32[]{:S(2)}) %collective-permute-start.7) | collective-permute-done | bytes 327712 | tf_op jit(solution)/shard_map/ppermute | solution.py:310
  52.8 5.4 %collective-permute-done.8.refs_9_.refs_1_ = bf16[8,160,128]{2,1,0:T(8,128)(2,1)S(1)} collective-permute-done((bf16[8,160,128]{2,1,0:T(8,128)(2,1)S(1)}, bf16[8,160,128]{2,1,0:T(8,128)(2,1)S(1)}, u32[]{:S(2)}, u32[]{:S(2)}) %collective-permute-start.8) | collective-permute-done | bytes 327712 | tf_op jit(solution)/shard_map/ppermute | solution.py:310
  60.9 3.1 %shard_map.69 = (bf16[16,128,128]{2,1,0:T(8,128)(2,1)S(1)}, bf16[16,128,128]{2,1,0:T(8,128)(2,1)S(1)}) custom-call(s32[256]{0:T(256)S(1)} %copy-done.2, bf16[16,160,128]{2,1,0:T(8,128)(2,1)S(1)} %shard_map.59.refs_0_, bf16[16,160,128]{2,1,0:T(8,128)(2,1)S(1)} %collective-permute-done.2.refs_0_.refs_1_, ...), custom_call_target="tpu_custom_call" | custom-call | bytes 6291456 | tf_op jit(solution)/shard_map/pallas_call | solution.py:251
  64.8 6.2 %shard_map.74 = (f32[2,32,640]{2,1,0:T(8,128)S(1)}, bf16[2,32,640]{2,1,0:T(8,128)(2,1)S(1)}, bf16[2,32,640]{2,1,0:T(8,128)(2,1)S(1)}, bf16[2,32,640]{2,1,0:T(8,1...) custom-call(bf16[160,16384]{1,0:T(8,128)(2,1)S(1)} %shard_map.60.ref, ...), custom_call_target="tpu_custom_call" | custom-call | flops 5368709120 | bytes 29360128 | tf_op jit(solution)/shard_map/pallas_call | solution.py:201
  71.7 1.6 %collective-permute-start.19 = (bf16[2,32,640]{2,1,0:T(8,128)(2,1)S(1)}, bf16[2,32,640]{2,1,0:T(8,128)(2,1)S(1)}, u32[]{:S(2)}, u32[]{:S(2)}) collective-permute-start(bf16[2,32,640]{2,1,0:T(8,128)(2,1)S(1)} %get-tuple-element.54), channel_id=1, source_target_pairs={{0,32},{16,48},{32,64},{48,80},{64,96},{80,112},{96,0},{112,16},{1... | collective-permute-start | bytes 245768 | tf_op jit(solution)/shard_map/ppermute | solution.py:349
  73.2 2.5 %collective-permute-start.20 = (bf16[2,32,640]{2,1,0:T(8,128)(2,1)S(1)}, bf16[2,32,640]{2,1,0:T(8,128)(2,1)S(1)}, u32[]{:S(2)}, u32[]{:S(2)}) collective-permute-start(bf16[2,32,640]{2,1,0:T(8,128)(2,1)S(1)} %get-tuple-element.55), channel_id=1, source_target_pairs={{0,48},{16,32},{32,80},{48,64},{64,112},{80,96},{96,16},{112,0},{1... | collective-permute-start | bytes 245768 | tf_op jit(solution)/shard_map/ppermute | solution.py:349
  75.7 1.5 %collective-permute-start.21 = (bf16[2,32,640]{2,1,0:T(8,128)(2,1)S(1)}, bf16[2,32,640]{2,1,0:T(8,128)(2,1)S(1)}, u32[]{:S(2)}, u32[]{:S(2)}) collective-permute-start(bf16[2,32,640]{2,1,0:T(8,128)(2,1)S(1)} %get-tuple-element.56), channel_id=1, source_target_pairs={{0,64},{16,80},{32,96},{48,112},{64,0},{80,16},{96,32},{112,48},{1... | collective-permute-start | bytes 245768 | tf_op jit(solution)/shard_map/ppermute | solution.py:349
  77.2 2.0 %collective-permute-start.22 = (bf16[2,32,640]{2,1,0:T(8,128)(2,1)S(1)}, bf16[2,32,640]{2,1,0:T(8,128)(2,1)S(1)}, u32[]{:S(2)}, u32[]{:S(2)}) collective-permute-start(bf16[2,32,640]{2,1,0:T(8,128)(2,1)S(1)} %get-tuple-element.57), channel_id=1, source_target_pairs={{0,80},{16,64},{32,112},{48,96},{64,16},{80,0},{96,48},{112,32},{1... | collective-permute-start | bytes 245768 | tf_op jit(solution)/shard_map/ppermute | solution.py:349
  79.2 1.7 %collective-permute-start.23 = (bf16[2,32,640]{2,1,0:T(8,128)(2,1)S(1)}, bf16[2,32,640]{2,1,0:T(8,128)(2,1)S(1)}, u32[]{:S(2)}, u32[]{:S(2)}) collective-permute-start(bf16[2,32,640]{2,1,0:T(8,128)(2,1)S(1)} %get-tuple-element.58), channel_id=1, source_target_pairs={{0,96},{16,112},{32,0},{48,16},{64,32},{80,48},{96,64},{112,80},{1... | collective-permute-start | bytes 245768 | tf_op jit(solution)/shard_map/ppermute | solution.py:349
  80.9 2.3 %collective-permute-start.24 = (bf16[2,32,640]{2,1,0:T(8,128)(2,1)S(1)}, bf16[2,32,640]{2,1,0:T(8,128)(2,1)S(1)}, u32[]{:S(2)}, u32[]{:S(2)}) collective-permute-start(bf16[2,32,640]{2,1,0:T(8,128)(2,1)S(1)} %get-tuple-element.59), channel_id=1, source_target_pairs={{0,112},{16,96},{32,16},{48,0},{64,48},{80,32},{96,80},{112,64},{1... | collective-permute-start | bytes 245768 | tf_op jit(solution)/shard_map/ppermute | solution.py:349
  83.2 1.7 %collective-permute-done.22.refs_5_ = bf16[2,32,640]{2,1,0:T(8,128)(2,1)S(1)} collective-permute-done((bf16[2,32,640]{2,1,0:T(8,128)(2,1)S(1)}, bf16[2,32,640]{2,1,0:T(8,128)(2,1)S(1)}, u32[]{:S(2)}, u32[]{:S(2)}) %collective-permute-start.22) | collective-permute-done | bytes 81952 | tf_op jit(solution)/shard_map/ppermute | solution.py:349
  86.3 1.5 %shard_map.75 = (bf16[16,128,128]{2,1,0:T(8,128)(2,1)}, f32[2,32,640]{2,1,0:T(8,128)}) custom-call(s32[256]{0:T(256)S(1)} %copy-done.2, bf16[16,128,128]{2,1,0:T(8,128)(2,1)S(1)} %get-tuple-element.49.mine_ref, bf16[16,128,128]{2,1,0:T(8,128)(2,1)S(1)} %collective-permute-done.13.theirs_ref, f32[2,32,640]{2,1,0:T(8,128)S(1)} %get-tuple-element.52.refs_0_, ...), custom_call_target="tpu_custom_call" | custom-call | bytes 3145728 | tf_op jit(solution)/shard_map/pallas_call | solution.py:280
  (51 shorter events, 15.9 us)
Async XLA Ops:
  2.9 18.4 %collective-permute-start.2 = (bf16[16,160,128]{2,1,0:T(8,128)(2,1)S(1)}, bf16[16,160,128]{2,1,0:T(8,128)(2,1)S(1)}, u32[]{:S(2)}, u32[]{:S(2)}) collective-permute-start(bf16[16,160,128]{2,1,0:T(8,128)(2,1)S(1)} %shard_map.59.refs_0_), channel_id=1, source_target_pairs={{0,8},{1,9},{2,10},{3,11},{4,12},{5,13},{6,14},{7,15},{8,0},{9,1},... | collective-permute-start | bytes 1966088 | tf_op jit(solution)/shard_map/ppermute | solution.py:310
  6.1 17.7 %collective-permute-start.1 = (bf16[16,160,128]{2,1,0:T(8,128)(2,1)S(1)}, bf16[16,160,128]{2,1,0:T(8,128)(2,1)S(1)}, u32[]{:S(2)}, u32[]{:S(2)}) collective-permute-start(bf16[16,160,128]{2,1,0:T(8,128)(2,1)S(1)} %shard_map.59.refs_0_), channel_id=1, source_target_pairs={{0,6},{1,7},{2,0},{3,1},{4,2},{5,3},{6,4},{7,5},{8,14},{9,15},{10,... | collective-permute-start | bytes 1966088 | tf_op jit(solution)/shard_map/ppermute | solution.py:310
  10.1 17.1 %collective-permute-start = (bf16[16,160,128]{2,1,0:T(8,128)(2,1)S(1)}, bf16[16,160,128]{2,1,0:T(8,128)(2,1)S(1)}, u32[]{:S(2)}, u32[]{:S(2)}) collective-permute-start(bf16[16,160,128]{2,1,0:T(8,128)(2,1)S(1)} %shard_map.59.refs_0_), channel_id=1, source_target_pairs={{0,2},{1,3},{2,4},{3,5},{4,6},{5,7},{6,0},{7,1},{8,10},{9,11},{10,... | collective-permute-start | bytes 1966088 | tf_op jit(solution)/shard_map/ppermute | solution.py:310
  27.3 8.0 %collective-permute-start.4 = (bf16[8,160,128]{2,1,0:T(8,128)(2,1)S(1)}, bf16[8,160,128]{2,1,0:T(8,128)(2,1)S(1)}, u32[]{:S(2)}, u32[]{:S(2)}) collective-permute-start(bf16[8,160,128]{2,1,0:T(8,128)(2,1)S(1)} %slice.7), channel_id=1, source_target_pairs={{0,6},{1,7},{2,0},{3,1},{4,2},{5,3},{6,4},{7,5},{8,14},{9,15},{10,... | collective-permute-start | bytes 983048 | tf_op jit(solution)/shard_map/ppermute | solution.py:310
  27.7 9.2 %collective-permute-start.3 = (bf16[8,160,128]{2,1,0:T(8,128)(2,1)S(1)}, bf16[8,160,128]{2,1,0:T(8,128)(2,1)S(1)}, u32[]{:S(2)}, u32[]{:S(2)}) collective-permute-start(bf16[8,160,128]{2,1,0:T(8,128)(2,1)S(1)} %slice.6), channel_id=1, source_target_pairs={{0,2},{1,3},{2,4},{3,5},{4,6},{5,7},{6,0},{7,1},{8,10},{9,11},{10,... | collective-permute-start | bytes 983048 | tf_op jit(solution)/shard_map/ppermute | solution.py:310
  36.9 3.7 %collective-permute-start.10 = (bf16[16,16384]{1,0:T(8,128)(2,1)S(1)}, bf16[16,16384]{1,0:T(8,128)(2,1)S(1)}, u32[]{:S(2)}, u32[]{:S(2)}) collective-permute-start(bf16[16,16384]{1,0:T(8,128)(2,1)S(1)} %shard_map.65.refs_5_), channel_id=1, source_target_pairs={{0,1},{1,0},{2,3},{3,2},{4,5},{5,4},{6,7},{7,6},{8,9},{9,8},{10,11... | collective-permute-start | bytes 1572872 | tf_op jit(solution)/shard_map/ppermute | solution.py:310
  37.4 4.2 %collective-permute-start.11 = (bf16[16,16384]{1,0:T(8,128)(2,1)S(1)}, bf16[16,16384]{1,0:T(8,128)(2,1)S(1)}, u32[]{:S(2)}, u32[]{:S(2)}) collective-permute-start(bf16[16,16384]{1,0:T(8,128)(2,1)S(1)} %shard_map.66.refs_6_), channel_id=1, source_target_pairs={{0,1},{1,0},{2,3},{3,2},{4,5},{5,4},{6,7},{7,6},{8,9},{9,8},{10,11... | collective-permute-start | bytes 1572872 | tf_op jit(solution)/shard_map/ppermute | solution.py:310
  37.4 6.8 %collective-permute-start.12 = (bf16[16,16384]{1,0:T(8,128)(2,1)S(1)}, bf16[16,16384]{1,0:T(8,128)(2,1)S(1)}, u32[]{:S(2)}, u32[]{:S(2)}) collective-permute-start(bf16[16,16384]{1,0:T(8,128)(2,1)S(1)} %shard_map.67.refs_7_), channel_id=1, source_target_pairs={{0,1},{1,0},{2,3},{3,2},{4,5},{5,4},{6,7},{7,6},{8,9},{9,8},{10,11... | collective-permute-start | bytes 1572872 | tf_op jit(solution)/shard_map/ppermute | solution.py:310
  37.9 20.4 %collective-permute-start.6 = (bf16[16,160,128]{2,1,0:T(8,128)(2,1)S(1)}, bf16[16,160,128]{2,1,0:T(8,128)(2,1)S(1)}, u32[]{:S(2)}, u32[]{:S(2)}) collective-permute-start(bf16[16,160,128]{2,1,0:T(8,128)(2,1)S(1)} %collective-permute-done.2.refs_0_.refs_1_), channel_id=1, source_target_pairs={{0,6},{1,7},{2,0},{3,1},{4,2},{5,3},{6,4},{7,5},{8,14},{9,15},{10,... | collective-permute-start | bytes 1966088 | tf_op jit(solution)/shard_map/ppermute | solution.py:310
  38.8 19.5 %collective-permute-start.5 = (bf16[16,160,128]{2,1,0:T(8,128)(2,1)S(1)}, bf16[16,160,128]{2,1,0:T(8,128)(2,1)S(1)}, u32[]{:S(2)}, u32[]{:S(2)}) collective-permute-start(bf16[16,160,128]{2,1,0:T(8,128)(2,1)S(1)} %collective-permute-done.2.refs_0_.refs_1_), channel_id=1, source_target_pairs={{0,2},{1,3},{2,4},{3,5},{4,6},{5,7},{6,0},{7,1},{8,10},{9,11},{10,... | collective-permute-start | bytes 1966088 | tf_op jit(solution)/shard_map/ppermute | solution.py:310
  40.6 12.2 %collective-permute-start.7 = (bf16[8,160,128]{2,1,0:T(8,128)(2,1)S(1)}, bf16[8,160,128]{2,1,0:T(8,128)(2,1)S(1)}, u32[]{:S(2)}, u32[]{:S(2)}) collective-permute-start(bf16[8,160,128]{2,1,0:T(8,128)(2,1)S(1)} %collective-permute-done.3.refs_4_.refs_0_), channel_id=1, source_target_pairs={{0,8},{1,9},{2,10},{3,11},{4,12},{5,13},{6,14},{7,15},{8,0},{9,1},... | collective-permute-start | bytes 983048 | tf_op jit(solution)/shard_map/ppermute | solution.py:310
  41.6 16.7 %collective-permute-start.8 = (bf16[8,160,128]{2,1,0:T(8,128)(2,1)S(1)}, bf16[8,160,128]{2,1,0:T(8,128)(2,1)S(1)}, u32[]{:S(2)}, u32[]{:S(2)}) collective-permute-start(bf16[8,160,128]{2,1,0:T(8,128)(2,1)S(1)} %collective-permute-done.4.refs_5_.refs_1_), channel_id=1, source_target_pairs={{0,8},{1,9},{2,10},{3,11},{4,12},{5,13},{6,14},{7,15},{8,0},{9,1},... | collective-permute-start | bytes 983048 | tf_op jit(solution)/shard_map/ppermute | solution.py:310
  44.2 20.6 %collective-permute-start.14 = (bf16[16,16384]{1,0:T(8,128)(2,1)S(1)}, bf16[16,16384]{1,0:T(8,128)(2,1)S(1)}, u32[]{:S(2)}, u32[]{:S(2)}) collective-permute-start(bf16[16,16384]{1,0:T(8,128)(2,1)S(1)} %shard_map.70.refs_4_), channel_id=1, source_target_pairs={{0,1},{1,0},{2,3},{3,2},{4,5},{5,4},{6,7},{7,6},{8,9},{9,8},{10,11... | collective-permute-start | bytes 1572872 | tf_op jit(solution)/shard_map/ppermute | solution.py:310
  60.3 4.5 %collective-permute-start.17 = (bf16[16,16384]{1,0:T(8,128)(2,1)S(1)}, bf16[16,16384]{1,0:T(8,128)(2,1)S(1)}, u32[]{:S(2)}, u32[]{:S(2)}) collective-permute-start(bf16[16,16384]{1,0:T(8,128)(2,1)S(1)} %shard_map.73.refs_7_), channel_id=1, source_target_pairs={{0,1},{1,0},{2,3},{3,2},{4,5},{5,4},{6,7},{7,6},{8,9},{9,8},{10,11... | collective-permute-start | bytes 1572872 | tf_op jit(solution)/shard_map/ppermute | solution.py:310
  60.3 4.4 %collective-permute-start.16 = (bf16[16,16384]{1,0:T(8,128)(2,1)S(1)}, bf16[16,16384]{1,0:T(8,128)(2,1)S(1)}, u32[]{:S(2)}, u32[]{:S(2)}) collective-permute-start(bf16[16,16384]{1,0:T(8,128)(2,1)S(1)} %shard_map.72.refs_6_), channel_id=1, source_target_pairs={{0,1},{1,0},{2,3},{3,2},{4,5},{5,4},{6,7},{7,6},{8,9},{9,8},{10,11... | collective-permute-start | bytes 1572872 | tf_op jit(solution)/shard_map/ppermute | solution.py:310
  60.8 3.9 %collective-permute-start.15 = (bf16[16,16384]{1,0:T(8,128)(2,1)S(1)}, bf16[16,16384]{1,0:T(8,128)(2,1)S(1)}, u32[]{:S(2)}, u32[]{:S(2)}) collective-permute-start(bf16[16,16384]{1,0:T(8,128)(2,1)S(1)} %shard_map.71.refs_5_), channel_id=1, source_target_pairs={{0,1},{1,0},{2,3},{3,2},{4,5},{5,4},{6,7},{7,6},{8,9},{9,8},{10,11... | collective-permute-start | bytes 1572872 | tf_op jit(solution)/shard_map/ppermute | solution.py:310
  64.1 13.2 %collective-permute-start.13 = (bf16[16,128,128]{2,1,0:T(8,128)(2,1)S(1)}, bf16[16,128,128]{2,1,0:T(8,128)(2,1)S(1)}, u32[]{:S(2)}, u32[]{:S(2)}) collective-permute-start(bf16[16,128,128]{2,1,0:T(8,128)(2,1)S(1)} %get-tuple-element.50), channel_id=1, source_target_pairs={{0,1},{1,0},{2,3},{3,2},{4,5},{5,4},{6,7},{7,6},{8,9},{9,8},{10,11... | collective-permute-start | bytes 1572872 | tf_op jit(solution)/shard_map/ppermute | solution.py:310
  71.0 8.3 %collective-permute-start.18 = (bf16[2,32,640]{2,1,0:T(8,128)(2,1)S(1)}, bf16[2,32,640]{2,1,0:T(8,128)(2,1)S(1)}, u32[]{:S(2)}, u32[]{:S(2)}) collective-permute-start(bf16[2,32,640]{2,1,0:T(8,128)(2,1)S(1)} %get-tuple-element.53), channel_id=1, source_target_pairs={{0,16},{16,0},{32,48},{48,32},{64,80},{80,64},{96,112},{112,96},{1... | collective-permute-start | bytes 245768 | tf_op jit(solution)/shard_map/ppermute | solution.py:349
  71.7 9.3 %collective-permute-start.19 = (bf16[2,32,640]{2,1,0:T(8,128)(2,1)S(1)}, bf16[2,32,640]{2,1,0:T(8,128)(2,1)S(1)}, u32[]{:S(2)}, u32[]{:S(2)}) collective-permute-start(bf16[2,32,640]{2,1,0:T(8,128)(2,1)S(1)} %get-tuple-element.54), channel_id=1, source_target_pairs={{0,32},{16,48},{32,64},{48,80},{64,96},{80,112},{96,0},{112,16},{1... | collective-permute-start | bytes 245768 | tf_op jit(solution)/shard_map/ppermute | solution.py:349
  73.2 10.0 %collective-permute-start.20 = (bf16[2,32,640]{2,1,0:T(8,128)(2,1)S(1)}, bf16[2,32,640]{2,1,0:T(8,128)(2,1)S(1)}, u32[]{:S(2)}, u32[]{:S(2)}) collective-permute-start(bf16[2,32,640]{2,1,0:T(8,128)(2,1)S(1)} %get-tuple-element.55), channel_id=1, source_target_pairs={{0,48},{16,32},{32,80},{48,64},{64,112},{80,96},{96,16},{112,0},{1... | collective-permute-start | bytes 245768 | tf_op jit(solution)/shard_map/ppermute | solution.py:349
  75.7 7.5 %collective-permute-start.21 = (bf16[2,32,640]{2,1,0:T(8,128)(2,1)S(1)}, bf16[2,32,640]{2,1,0:T(8,128)(2,1)S(1)}, u32[]{:S(2)}, u32[]{:S(2)}) collective-permute-start(bf16[2,32,640]{2,1,0:T(8,128)(2,1)S(1)} %get-tuple-element.56), channel_id=1, source_target_pairs={{0,64},{16,80},{32,96},{48,112},{64,0},{80,16},{96,32},{112,48},{1... | collective-permute-start | bytes 245768 | tf_op jit(solution)/shard_map/ppermute | solution.py:349
  77.2 7.7 %collective-permute-start.22 = (bf16[2,32,640]{2,1,0:T(8,128)(2,1)S(1)}, bf16[2,32,640]{2,1,0:T(8,128)(2,1)S(1)}, u32[]{:S(2)}, u32[]{:S(2)}) collective-permute-start(bf16[2,32,640]{2,1,0:T(8,128)(2,1)S(1)} %get-tuple-element.57), channel_id=1, source_target_pairs={{0,80},{16,64},{32,112},{48,96},{64,16},{80,0},{96,48},{112,32},{1... | collective-permute-start | bytes 245768 | tf_op jit(solution)/shard_map/ppermute | solution.py:349
  79.2 6.2 %collective-permute-start.23 = (bf16[2,32,640]{2,1,0:T(8,128)(2,1)S(1)}, bf16[2,32,640]{2,1,0:T(8,128)(2,1)S(1)}, u32[]{:S(2)}, u32[]{:S(2)}) collective-permute-start(bf16[2,32,640]{2,1,0:T(8,128)(2,1)S(1)} %get-tuple-element.58), channel_id=1, source_target_pairs={{0,96},{16,112},{32,0},{48,16},{64,32},{80,48},{96,64},{112,80},{1... | collective-permute-start | bytes 245768 | tf_op jit(solution)/shard_map/ppermute | solution.py:349
  80.9 5.4 %collective-permute-start.24 = (bf16[2,32,640]{2,1,0:T(8,128)(2,1)S(1)}, bf16[2,32,640]{2,1,0:T(8,128)(2,1)S(1)}, u32[]{:S(2)}, u32[]{:S(2)}) collective-permute-start(bf16[2,32,640]{2,1,0:T(8,128)(2,1)S(1)} %get-tuple-element.59), channel_id=1, source_target_pairs={{0,112},{16,96},{32,16},{48,0},{64,48},{80,32},{96,80},{112,64},{1... | collective-permute-start | bytes 245768 | tf_op jit(solution)/shard_map/ppermute | solution.py:349
  (4 other events, 20.9 us)

commit v3 on v2

--- a/solution.py
+++ b/solution.py
@@ -10,6 +10,7 @@
 BF = jnp.bfloat16
 F32 = jnp.float32
 WHOLE = pl.BlockSpec(memory_space=pltpu.VMEM)
+SHORT = pl.CostEstimate(flops=0, bytes_accessed=1024, transcendentals=0)
 
 
 def near(value):
@@ -63,28 +64,33 @@
             pltpu.SemaphoreType.DMA((count // 32,)),
         ],
         compiler_params=pltpu.CompilerParams(vmem_limit_bytes=10 << 20),
-        cost_estimate=pl.CostEstimate(
-            flops=2 * count * 16384 * 256, bytes_accessed=4 * count * 16384, transcendentals=0
-        ),
+        cost_estimate=SHORT,
     )(pltpu.with_memory_space_constraint(vectors, pltpu.HBM))
 
 
-def pack_kernel(walk_ref, inv_ref, out_ref):
-    out_ref[:, 0:128, :] = walk_ref[...]
+def pack_kernel(walk_ref, inv_ref, out_ref, held, came):
+    walk = pltpu.make_async_copy(walk_ref, out_ref.at[:, pl.ds(0, 128), :], came.at[0])
+    inverse = pltpu.make_async_copy(inv_ref, held, came.at[1])
+    inverse.start()
+    walk.start()
+    inverse.wait()
     for w in range(16):
-        blocks = [inv_ref[w, 32 * n : 32 * n + 32, :] for n in range(4)]
+        blocks = [held[w, 32 * n : 32 * n + 32, :] for n in range(4)]
         out_ref[w, 128:160, :] = jnp.concatenate(blocks, axis=1)
+    walk.wait()
 
 
 def pack(walkers, inverse):
+    inputs = [walkers, inverse.reshape(16, 128, 32)]
     return pl.pallas_call(
         pack_kernel,
-        in_specs=[WHOLE] * 2,
+        in_specs=[pl.BlockSpec(memory_space=pl.ANY)] * 2,
         out_specs=WHOLE,
         out_shape=pltpu.VMEM((16, 160, 128), BF),
+        scratch_shapes=[pltpu.VMEM((16, 128, 32), BF), pltpu.SemaphoreType.DMA((2,))],
         compiler_params=pltpu.CompilerParams(vmem_limit_bytes=6 << 20),
-        cost_estimate=pl.CostEstimate(flops=0, bytes_accessed=2 << 20, transcendentals=0),
-    )(walkers, inverse.reshape(16, 128, 32))
+        cost_estimate=SHORT,
+    )(*[pltpu.with_memory_space_constraint(a, pltpu.HBM) for a in inputs])
 
 
 def theta_kernel(*refs):
@@ -123,9 +129,7 @@
         out_shape=pltpu.VMEM((16, 16384), BF),
         scratch_shapes=[pltpu.VMEM((16, 128, 128), BF)],
         compiler_params=pltpu.CompilerParams(vmem_limit_bytes=6 << 20),
-        cost_estimate=pl.CostEstimate(
-            flops=2 * 16 * 16384 * 256, bytes_accessed=2 << 20, transcendentals=0
-        ),
+        cost_estimate=SHORT,
     )(*[near(piece) for piece in pieces])
 
 
@@ -205,9 +209,7 @@
         out_shape=shapes,
         scratch_shapes=[pltpu.VMEM((count, 256), F32)],
         compiler_params=pltpu.CompilerParams(vmem_limit_bytes=14 << 20),
-        cost_estimate=pl.CostEstimate(
-            flops=2 * count * 16384 * 256, bytes_accessed=2 * (count + 256) * 16384, transcendentals=0
-        ),
+        cost_estimate=SHORT,
     )(*operands)
 
 
@@ -259,7 +261,7 @@
         ],
         out_shape=[shape, shape],
         compiler_params=pltpu.CompilerParams(vmem_limit_bytes=8 << 20),
-        cost_estimate=pl.CostEstimate(flops=0, bytes_accessed=6 << 20, transcendentals=0),
+        cost_estimate=SHORT,
     )(sources, *[near(piece) for piece in pieces])
 
 
@@ -286,7 +288,7 @@
             jax.ShapeDtypeStruct(sums[0].shape, F32),
         ],
         compiler_params=pltpu.CompilerParams(vmem_limit_bytes=8 << 20),
-        cost_estimate=pl.CostEstimate(flops=0, bytes_accessed=3 << 20, transcendentals=0),
+        cost_estimate=SHORT,
     )(sources, *operands)
 
 
@@ -332,10 +334,12 @@
     short = sources.reshape(2, 128)
     operands = [t[0] for t in thetas[:4]] + [t[1] for t in thetas[:4]]
     sums = product(0, flats, operands, short, [])
-    second = [across_below, across_above, across_far]
+    second = [across_below, across_above]
     second, sums = after(second, sums)
-    across_below, across_above, across_far = second
-    more = [theta_of(across_below), theta_of(across_above), theta_of(*across_far)]
+    across_below, across_above = second
+    more = [theta_of(piece) for piece in second]
+    across_far, more = after(across_far, more)
+    more.append(theta_of(*across_far))
     thetas += [(t, send(t, OTHER)) for t in more]
     operands = [t[0] for t in thetas[4:]] + [t[1] for t in thetas[4:]]
     pieces = [own, across, below, above, *far, across_below, across_above, *across_far]

time: 88.1 us -> 85.1 us (0.966)
  waiting for transfers between devices: 19.6 us -> 15.9 us
  local copies, waits for them, and re-layouts: 2.13 us -> 0.05 us
  starting transfers between devices: 29 us -> 30.7 us
  Pallas kernels: 36.4 us -> 37.5 us
    ppermute x18, waiting for transfers between devices: 16.4 us -> 10.9 us  [send(): return lax.ppermute(value, 'walk', pairs)]
    ppermute x18, starting transfers between devices: 16.8 us -> 19.5 us  [send(): return lax.ppermute(value, 'walk', pairs)]
    unnamed x6 -> x2, local copies, waits for them, and re-layouts: 2.08 us -> 0.01 us
    ppermute x7, waiting for transfers between devices: 3.13 us -> 4.92 us  [per_device(): sums[k] = lax.ppermute(sums[k], 'vec', pairs)]
    pallas_call x1, Pallas kernels: 0.16 us -> 1.23 us  [pack(): pl.pallas_call(pack_kernel, in_specs=[pl.BlockSpec(memory_space=pl.ANY)]...]
    ppermute x7, starting transfers between devices: 12.2 us -> 11.2 us  [per_device(): sums[k] = lax.ppermute(sums[k], 'vec', pairs)]
  transfers between devices with their start and end apart: 25 -> 25, of which waited for: 10 -> 8; matrix products, arithmetic and copies ran while one was open for 0% -> 0% of each run, Pallas kernels for 39% -> 41%
where the time goes in v3:
time: 85.1 us; the launch traced here: 85 us
  Pallas kernels  37.5 us (44%)
  starting transfers between devices  30.7 us (36%)
  waiting for transfers between devices  15.9 us (19%)
    ppermute x18, starting transfers between devices, send(): return lax.ppermute(value, 'walk', pairs)  19.5 us
    pallas_call x4, Pallas kernels, flatten_vectors(): pl.pallas_call(functools.partial(flatten_kernel, start), in_specs=[pl.Blo...  13.9 us
    pallas_call x2, Pallas kernels, product(): pl.pallas_call(functools.partial(product_kernel, part), in_specs=[WHOLE]...  12.4 us
    ppermute x7, starting transfers between devices, per_device(): sums[k] = lax.ppermute(sums[k], 'vec', pairs)  11.2 us
    ppermute x18, waiting for transfers between devices, send(): return lax.ppermute(value, 'walk', pairs)  10.9 us
    pallas_call x8, Pallas kernels, theta_of(): pl.pallas_call(theta_kernel, in_specs=[WHOLE] * len(pieces), out_specs=WH...  5.29 us
    ppermute x7, waiting for transfers between devices, per_device(): sums[k] = lax.ppermute(sums[k], 'vec', pairs)  4.92 us
    pallas_call x1, Pallas kernels, choose(): pl.pallas_call(choose_kernel, in_specs=[pl.BlockSpec(memory_space=pltpu.S...  3.11 us
  transfers between devices with their start and end apart: 25, of which 8 were waited for; matrix products, arithmetic and copies ran while one was open for 0% of the time, Pallas kernels for 41%

profile of v3, /device:TPU:0, one launch (start us, length us, event | category | flops | bytes accessed | tf_op | source)
XLA Modules:
  0.0 85.0 jit_solution(5276560937188512359)
XLA Ops:
  1.9 2.1 %collective-permute-start = (bf16[16,160,128]{2,1,0:T(8,128)(2,1)S(1)}, bf16[16,160,128]{2,1,0:T(8,128)(2,1)S(1)}, u32[]{:S(2)}, u32[]{:S(2)}) collective-permute-start(bf16[16,160,128]{2,1,0:T(8,128)(2,1)S(1)} %shard_map.59.refs_0_), channel_id=1, source_target_pairs={{0,2},{1,3},{2,4},{3,5},{4,6},{5,7},{6,0},{7,1},{8,10},{9,11},{10,... | collective-permute-start | bytes 1966088 | tf_op jit(solution)/shard_map/ppermute | solution.py:312
  3.9 2.2 %collective-permute-start.1 = (bf16[16,160,128]{2,1,0:T(8,128)(2,1)S(1)}, bf16[16,160,128]{2,1,0:T(8,128)(2,1)S(1)}, u32[]{:S(2)}, u32[]{:S(2)}) collective-permute-start(bf16[16,160,128]{2,1,0:T(8,128)(2,1)S(1)} %shard_map.59.refs_0_), channel_id=1, source_target_pairs={{0,6},{1,7},{2,0},{3,1},{4,2},{5,3},{6,4},{7,5},{8,14},{9,15},{10,... | collective-permute-start | bytes 1966088 | tf_op jit(solution)/shard_map/ppermute | solution.py:312
  6.1 3.0 %collective-permute-start.2 = (bf16[16,160,128]{2,1,0:T(8,128)(2,1)S(1)}, bf16[16,160,128]{2,1,0:T(8,128)(2,1)S(1)}, u32[]{:S(2)}, u32[]{:S(2)}) collective-permute-start(bf16[16,160,128]{2,1,0:T(8,128)(2,1)S(1)} %shard_map.59.refs_0_), channel_id=1, source_target_pairs={{0,8},{1,9},{2,10},{3,11},{4,12},{5,13},{6,14},{7,15},{8,0},{9,1},... | collective-permute-start | bytes 1966088 | tf_op jit(solution)/shard_map/ppermute | solution.py:312
  9.2 3.5 %shard_map.60.refs_0_ = bf16[160,16384]{1,0:T(8,128)(2,1)S(1)} custom-call(bf16[640,128,128]{2,1,0:T(8,128)(2,1)} %v_ref.7), custom_call_target="tpu_custom_call" | custom-call | bytes 1024 | tf_op jit(solution)/shard_map/pallas_call | solution.py:57
  12.6 3.5 %shard_map.61.refs_1_ = bf16[160,16384]{1,0:T(8,128)(2,1)S(1)} custom-call(bf16[640,128,128]{2,1,0:T(8,128)(2,1)} %v_ref.7), custom_call_target="tpu_custom_call" | custom-call | bytes 1024 | tf_op jit(solution)/shard_map/pallas_call | solution.py:57
  16.1 3.5 %shard_map.62.refs_2_ = bf16[160,16384]{1,0:T(8,128)(2,1)S(1)} custom-call(bf16[640,128,128]{2,1,0:T(8,128)(2,1)} %v_ref.7), custom_call_target="tpu_custom_call" | custom-call | bytes 1024 | tf_op jit(solution)/shard_map/pallas_call | solution.py:57
  20.8 3.0 %collective-permute-done.2.refs_0_.refs_1_ = bf16[16,160,128]{2,1,0:T(8,128)(2,1)S(1)} collective-permute-done((bf16[16,160,128]{2,1,0:T(8,128)(2,1)S(1)}, bf16[16,160,128]{2,1,0:T(8,128)(2,1)S(1)}, u32[]{:S(2)}, u32[]{:S(2)}) %collective-permute-start.2) | collective-permute-done | bytes 655392 | tf_op jit(solution)/shard_map/ppermute | solution.py:312
  24.0 3.3 %collective-permute-start.4 = (bf16[8,160,128]{2,1,0:T(8,128)(2,1)S(1)}, bf16[8,160,128]{2,1,0:T(8,128)(2,1)S(1)}, u32[]{:S(2)}, u32[]{:S(2)}) collective-permute-start(bf16[8,160,128]{2,1,0:T(8,128)(2,1)S(1)} %slice.7), channel_id=1, source_target_pairs={{0,6},{1,7},{2,0},{3,1},{4,2},{5,3},{6,4},{7,5},{8,14},{9,15},{10,... | collective-permute-start | bytes 983048 | tf_op jit(solution)/shard_map/ppermute | solution.py:312
  27.3 3.5 %shard_map.64.refs_3_ = bf16[160,16384]{1,0:T(8,128)(2,1)S(1)} custom-call(bf16[640,128,128]{2,1,0:T(8,128)(2,1)} %v_ref.7), custom_call_target="tpu_custom_call" | custom-call | bytes 1024 | tf_op jit(solution)/shard_map/pallas_call | solution.py:57
  33.9 3.2 %collective-permute-start.6 = (bf16[16,160,128]{2,1,0:T(8,128)(2,1)S(1)}, bf16[16,160,128]{2,1,0:T(8,128)(2,1)S(1)}, u32[]{:S(2)}, u32[]{:S(2)}) collective-permute-start(bf16[16,160,128]{2,1,0:T(8,128)(2,1)S(1)} %collective-permute-done.2.refs_0_.refs_1_), channel_id=1, source_target_pairs={{0,6},{1,7},{2,0},{3,1},{4,2},{5,3},{6,4},{7,5},{8,14},{9,15},{10,... | collective-permute-start | bytes 1966088 | tf_op jit(solution)/shard_map/ppermute | solution.py:312
  37.2 3.1 %collective-permute-start.11 = (bf16[8,160,128]{2,1,0:T(8,128)(2,1)S(1)}, bf16[8,160,128]{2,1,0:T(8,128)(2,1)S(1)}, u32[]{:S(2)}, u32[]{:S(2)}) collective-permute-start(bf16[8,160,128]{2,1,0:T(8,128)(2,1)S(1)} %collective-permute-done.3.refs_4_.refs_0_), channel_id=1, source_target_pairs={{0,8},{1,9},{2,10},{3,11},{4,12},{5,13},{6,14},{7,15},{8,0},{9,1},... | collective-permute-start | bytes 983048 | tf_op jit(solution)/shard_map/ppermute | solution.py:312
  41.6 6.2 %shard_map.68.refs_13_ = f32[2,256,640]{2,1,0:T(8,128)S(1)} custom-call(bf16[160,16384]{1,0:T(8,128)(2,1)S(1)} %shard_map.60.refs_0_, bf16[160,16384]{1,0:T(8,128)(2,1)S(1)} %shard_map.61.refs_1_, bf16[160,16384]{1,0:T(8,128)(2,1)S(1)} %shard_map.62.refs_2_, bf16[160,16384]{1,0:T(8,128)(2,1)S(1)} %shard_map.64.refs_3_, ...), custom_call_target="tpu_custom_call" | custom-call | bytes 1024 | tf_op jit(solution)/shard_map/pallas_call | solution.py:205
  47.8 4.6 %collective-permute-done.5.refs_0_.refs_6_ = bf16[16,160,128]{2,1,0:T(8,128)(2,1)S(1)} collective-permute-done((bf16[16,160,128]{2,1,0:T(8,128)(2,1)S(1)}, bf16[16,160,128]{2,1,0:T(8,128)(2,1)S(1)}, u32[]{:S(2)}, u32[]{:S(2)}) %collective-permute-start.5) | collective-permute-done | bytes 655392 | tf_op jit(solution)/shard_map/ppermute | solution.py:312
  53.7 2.1 %collective-permute-done.12.refs_9_.refs_1_ = bf16[8,160,128]{2,1,0:T(8,128)(2,1)S(1)} collective-permute-done((bf16[8,160,128]{2,1,0:T(8,128)(2,1)S(1)}, bf16[8,160,128]{2,1,0:T(8,128)(2,1)S(1)}, u32[]{:S(2)}, u32[]{:S(2)}) %collective-permute-start.12) | collective-permute-done | bytes 327712 | tf_op jit(solution)/shard_map/ppermute | solution.py:312
  57.1 3.1 %shard_map.71 = (bf16[16,128,128]{2,1,0:T(8,128)(2,1)S(1)}, bf16[16,128,128]{2,1,0:T(8,128)(2,1)S(1)}) custom-call(s32[256]{0:T(256)S(1)} %copy-done, bf16[16,160,128]{2,1,0:T(8,128)(2,1)S(1)} %shard_map.59.refs_0_, bf16[16,160,128]{2,1,0:T(8,128)(2,1)S(1)} %collective-permute-done.2.refs_0_.refs_1_, ...), custom_call_target="tpu_custom_call" | custom-call | bytes 1024 | tf_op jit(solution)/shard_map/pallas_call | solution.py:253
  61.0 6.2 %shard_map.74 = (f32[2,32,640]{2,1,0:T(8,128)S(1)}, bf16[2,32,640]{2,1,0:T(8,128)(2,1)S(1)}, bf16[2,32,640]{2,1,0:T(8,128)(2,1)S(1)}, bf16[2,32,640]{2,1,0:T(8,1...) custom-call(bf16[160,16384]{1,0:T(8,128)(2,1)S(1)} %shard_map.60.ref, ...), custom_call_target="tpu_custom_call" | custom-call | bytes 1024 | tf_op jit(solution)/shard_map/pallas_call | solution.py:205
  67.3 1.6 %collective-permute-start.18 = (bf16[2,32,640]{2,1,0:T(8,128)(2,1)S(1)}, bf16[2,32,640]{2,1,0:T(8,128)(2,1)S(1)}, u32[]{:S(2)}, u32[]{:S(2)}) collective-permute-start(bf16[2,32,640]{2,1,0:T(8,128)(2,1)S(1)} %get-tuple-element.57), channel_id=1, source_target_pairs={{0,16},{16,0},{32,48},{48,32},{64,80},{80,64},{96,112},{112,96},{1... | collective-permute-start | bytes 245768 | tf_op jit(solution)/shard_map/ppermute | solution.py:353
  68.8 1.6 %collective-permute-start.19 = (bf16[2,32,640]{2,1,0:T(8,128)(2,1)S(1)}, bf16[2,32,640]{2,1,0:T(8,128)(2,1)S(1)}, u32[]{:S(2)}, u32[]{:S(2)}) collective-permute-start(bf16[2,32,640]{2,1,0:T(8,128)(2,1)S(1)} %get-tuple-element.58), channel_id=1, source_target_pairs={{0,32},{16,48},{32,64},{48,80},{64,96},{80,112},{96,0},{112,16},{1... | collective-permute-start | bytes 245768 | tf_op jit(solution)/shard_map/ppermute | solution.py:353
  72.0 1.6 %collective-permute-start.21 = (bf16[2,32,640]{2,1,0:T(8,128)(2,1)S(1)}, bf16[2,32,640]{2,1,0:T(8,128)(2,1)S(1)}, u32[]{:S(2)}, u32[]{:S(2)}) collective-permute-start(bf16[2,32,640]{2,1,0:T(8,128)(2,1)S(1)} %get-tuple-element.60), channel_id=1, source_target_pairs={{0,64},{16,80},{32,96},{48,112},{64,0},{80,16},{96,32},{112,48},{1... | collective-permute-start | bytes 245768 | tf_op jit(solution)/shard_map/ppermute | solution.py:353
  73.5 2.9 %collective-permute-start.22 = (bf16[2,32,640]{2,1,0:T(8,128)(2,1)S(1)}, bf16[2,32,640]{2,1,0:T(8,128)(2,1)S(1)}, u32[]{:S(2)}, u32[]{:S(2)}) collective-permute-start(bf16[2,32,640]{2,1,0:T(8,128)(2,1)S(1)} %get-tuple-element.61), channel_id=1, source_target_pairs={{0,80},{16,64},{32,112},{48,96},{64,16},{80,0},{96,48},{112,32},{1... | collective-permute-start | bytes 245768 | tf_op jit(solution)/shard_map/ppermute | solution.py:353
  76.4 1.7 %collective-permute-start.23 = (bf16[2,32,640]{2,1,0:T(8,128)(2,1)S(1)}, bf16[2,32,640]{2,1,0:T(8,128)(2,1)S(1)}, u32[]{:S(2)}, u32[]{:S(2)}) collective-permute-start(bf16[2,32,640]{2,1,0:T(8,128)(2,1)S(1)} %get-tuple-element.62), channel_id=1, source_target_pairs={{0,96},{16,112},{32,0},{48,16},{64,32},{80,48},{96,64},{112,80},{1... | collective-permute-start | bytes 245768 | tf_op jit(solution)/shard_map/ppermute | solution.py:353
  78.5 2.2 %collective-permute-done.21.refs_4_ = bf16[2,32,640]{2,1,0:T(8,128)(2,1)S(1)} collective-permute-done((bf16[2,32,640]{2,1,0:T(8,128)(2,1)S(1)}, bf16[2,32,640]{2,1,0:T(8,128)(2,1)S(1)}, u32[]{:S(2)}, u32[]{:S(2)}) %collective-permute-start.21) | collective-permute-done | bytes 81952 | tf_op jit(solution)/shard_map/ppermute | solution.py:353
  81.8 1.6 %collective-permute-done.24.refs_7_ = bf16[2,32,640]{2,1,0:T(8,128)(2,1)S(1)} collective-permute-done((bf16[2,32,640]{2,1,0:T(8,128)(2,1)S(1)}, bf16[2,32,640]{2,1,0:T(8,128)(2,1)S(1)}, u32[]{:S(2)}, u32[]{:S(2)}) %collective-permute-start.24) | collective-permute-done | bytes 81952 | tf_op jit(solution)/shard_map/ppermute | solution.py:353
  83.4 1.6 %shard_map.75 = (bf16[16,128,128]{2,1,0:T(8,128)(2,1)}, f32[2,32,640]{2,1,0:T(8,128)}) custom-call(s32[256]{0:T(256)S(1)} %copy-done, bf16[16,128,128]{2,1,0:T(8,128)(2,1)S(1)} %get-tuple-element.51.mine_ref, bf16[16,128,128]{2,1,0:T(8,128)(2,1)S(1)} %collective-permute-done.13.theirs_ref, f32[2,32,640]{2,1,0:T(8,128)S(1)} %get-tuple-element.56.refs_0_, ...), custom_call_target="tpu_custom_call" | custom-call | bytes 1024 | tf_op jit(solution)/shard_map/pallas_call | solution.py:282
  (47 shorter events, 13.5 us)
Async XLA Ops:
  1.9 18.9 %collective-permute-start = (bf16[16,160,128]{2,1,0:T(8,128)(2,1)S(1)}, bf16[16,160,128]{2,1,0:T(8,128)(2,1)S(1)}, u32[]{:S(2)}, u32[]{:S(2)}) collective-permute-start(bf16[16,160,128]{2,1,0:T(8,128)(2,1)S(1)} %shard_map.59.refs_0_), channel_id=1, source_target_pairs={{0,2},{1,3},{2,4},{3,5},{4,6},{5,7},{6,0},{7,1},{8,10},{9,11},{10,... | collective-permute-start | bytes 1966088 | tf_op jit(solution)/shard_map/ppermute | solution.py:312
  3.9 16.9 %collective-permute-start.1 = (bf16[16,160,128]{2,1,0:T(8,128)(2,1)S(1)}, bf16[16,160,128]{2,1,0:T(8,128)(2,1)S(1)}, u32[]{:S(2)}, u32[]{:S(2)}) collective-permute-start(bf16[16,160,128]{2,1,0:T(8,128)(2,1)S(1)} %shard_map.59.refs_0_), channel_id=1, source_target_pairs={{0,6},{1,7},{2,0},{3,1},{4,2},{5,3},{6,4},{7,5},{8,14},{9,15},{10,... | collective-permute-start | bytes 1966088 | tf_op jit(solution)/shard_map/ppermute | solution.py:312
  6.1 17.7 %collective-permute-start.2 = (bf16[16,160,128]{2,1,0:T(8,128)(2,1)S(1)}, bf16[16,160,128]{2,1,0:T(8,128)(2,1)S(1)}, u32[]{:S(2)}, u32[]{:S(2)}) collective-permute-start(bf16[16,160,128]{2,1,0:T(8,128)(2,1)S(1)} %shard_map.59.refs_0_), channel_id=1, source_target_pairs={{0,8},{1,9},{2,10},{3,11},{4,12},{5,13},{6,14},{7,15},{8,0},{9,1},... | collective-permute-start | bytes 1966088 | tf_op jit(solution)/shard_map/ppermute | solution.py:312
  23.9 9.5 %collective-permute-start.3 = (bf16[8,160,128]{2,1,0:T(8,128)(2,1)S(1)}, bf16[8,160,128]{2,1,0:T(8,128)(2,1)S(1)}, u32[]{:S(2)}, u32[]{:S(2)}) collective-permute-start(bf16[8,160,128]{2,1,0:T(8,128)(2,1)S(1)} %slice.6), channel_id=1, source_target_pairs={{0,2},{1,3},{2,4},{3,5},{4,6},{5,7},{6,0},{7,1},{8,10},{9,11},{10,... | collective-permute-start | bytes 983048 | tf_op jit(solution)/shard_map/ppermute | solution.py:312
  24.0 9.4 %collective-permute-start.4 = (bf16[8,160,128]{2,1,0:T(8,128)(2,1)S(1)}, bf16[8,160,128]{2,1,0:T(8,128)(2,1)S(1)}, u32[]{:S(2)}, u32[]{:S(2)}) collective-permute-start(bf16[8,160,128]{2,1,0:T(8,128)(2,1)S(1)} %slice.7), channel_id=1, source_target_pairs={{0,6},{1,7},{2,0},{3,1},{4,2},{5,3},{6,4},{7,5},{8,14},{9,15},{10,... | collective-permute-start | bytes 983048 | tf_op jit(solution)/shard_map/ppermute | solution.py:312
  33.4 3.8 %collective-permute-start.8 = (bf16[16,16384]{1,0:T(8,128)(2,1)S(1)}, bf16[16,16384]{1,0:T(8,128)(2,1)S(1)}, u32[]{:S(2)}, u32[]{:S(2)}) collective-permute-start(bf16[16,16384]{1,0:T(8,128)(2,1)S(1)} %shard_map.65.refs_5_), channel_id=1, source_target_pairs={{0,1},{1,0},{2,3},{3,2},{4,5},{5,4},{6,7},{7,6},{8,9},{9,8},{10,11... | collective-permute-start | bytes 1572872 | tf_op jit(solution)/shard_map/ppermute | solution.py:312
  33.9 6.4 %collective-permute-start.9 = (bf16[16,16384]{1,0:T(8,128)(2,1)S(1)}, bf16[16,16384]{1,0:T(8,128)(2,1)S(1)}, u32[]{:S(2)}, u32[]{:S(2)}) collective-permute-start(bf16[16,16384]{1,0:T(8,128)(2,1)S(1)} %shard_map.66.refs_6_), channel_id=1, source_target_pairs={{0,1},{1,0},{2,3},{3,2},{4,5},{5,4},{6,7},{7,6},{8,9},{9,8},{10,11... | collective-permute-start | bytes 1572872 | tf_op jit(solution)/shard_map/ppermute | solution.py:312
  33.9 18.5 %collective-permute-start.5 = (bf16[16,160,128]{2,1,0:T(8,128)(2,1)S(1)}, bf16[16,160,128]{2,1,0:T(8,128)(2,1)S(1)}, u32[]{:S(2)}, u32[]{:S(2)}) collective-permute-start(bf16[16,160,128]{2,1,0:T(8,128)(2,1)S(1)} %collective-permute-done.2.refs_0_.refs_1_), channel_id=1, source_target_pairs={{0,2},{1,3},{2,4},{3,5},{4,6},{5,7},{6,0},{7,1},{8,10},{9,11},{10,... | collective-permute-start | bytes 1966088 | tf_op jit(solution)/shard_map/ppermute | solution.py:312
  33.9 18.5 %collective-permute-start.6 = (bf16[16,160,128]{2,1,0:T(8,128)(2,1)S(1)}, bf16[16,160,128]{2,1,0:T(8,128)(2,1)S(1)}, u32[]{:S(2)}, u32[]{:S(2)}) collective-permute-start(bf16[16,160,128]{2,1,0:T(8,128)(2,1)S(1)} %collective-permute-done.2.refs_0_.refs_1_), channel_id=1, source_target_pairs={{0,6},{1,7},{2,0},{3,1},{4,2},{5,3},{6,4},{7,5},{8,14},{9,15},{10,... | collective-permute-start | bytes 1966088 | tf_op jit(solution)/shard_map/ppermute | solution.py:312
  37.2 4.3 %collective-permute-start.10 = (bf16[16,16384]{1,0:T(8,128)(2,1)S(1)}, bf16[16,16384]{1,0:T(8,128)(2,1)S(1)}, u32[]{:S(2)}, u32[]{:S(2)}) collective-permute-start(bf16[16,16384]{1,0:T(8,128)(2,1)S(1)} %shard_map.67.refs_7_), channel_id=1, source_target_pairs={{0,1},{1,0},{2,3},{3,2},{4,5},{5,4},{6,7},{7,6},{8,9},{9,8},{10,11... | collective-permute-start | bytes 1572872 | tf_op jit(solution)/shard_map/ppermute | solution.py:312
  37.2 16.5 %collective-permute-start.11 = (bf16[8,160,128]{2,1,0:T(8,128)(2,1)S(1)}, bf16[8,160,128]{2,1,0:T(8,128)(2,1)S(1)}, u32[]{:S(2)}, u32[]{:S(2)}) collective-permute-start(bf16[8,160,128]{2,1,0:T(8,128)(2,1)S(1)} %collective-permute-done.3.refs_4_.refs_0_), channel_id=1, source_target_pairs={{0,8},{1,9},{2,10},{3,11},{4,12},{5,13},{6,14},{7,15},{8,0},{9,1},... | collective-permute-start | bytes 983048 | tf_op jit(solution)/shard_map/ppermute | solution.py:312
  40.3 15.6 %collective-permute-start.12 = (bf16[8,160,128]{2,1,0:T(8,128)(2,1)S(1)}, bf16[8,160,128]{2,1,0:T(8,128)(2,1)S(1)}, u32[]{:S(2)}, u32[]{:S(2)}) collective-permute-start(bf16[8,160,128]{2,1,0:T(8,128)(2,1)S(1)} %collective-permute-done.4.refs_5_.refs_1_), channel_id=1, source_target_pairs={{0,8},{1,9},{2,10},{3,11},{4,12},{5,13},{6,14},{7,15},{8,0},{9,1},... | collective-permute-start | bytes 983048 | tf_op jit(solution)/shard_map/ppermute | solution.py:312
  41.5 19.6 %collective-permute-start.14 = (bf16[16,16384]{1,0:T(8,128)(2,1)S(1)}, bf16[16,16384]{1,0:T(8,128)(2,1)S(1)}, u32[]{:S(2)}, u32[]{:S(2)}) collective-permute-start(bf16[16,16384]{1,0:T(8,128)(2,1)S(1)} %shard_map.72.refs_4_), channel_id=1, source_target_pairs={{0,1},{1,0},{2,3},{3,2},{4,5},{5,4},{6,7},{7,6},{8,9},{9,8},{10,11... | collective-permute-start | bytes 1572872 | tf_op jit(solution)/shard_map/ppermute | solution.py:312
  55.8 5.2 %collective-permute-start.15 = (bf16[16,16384]{1,0:T(8,128)(2,1)S(1)}, bf16[16,16384]{1,0:T(8,128)(2,1)S(1)}, u32[]{:S(2)}, u32[]{:S(2)}) collective-permute-start(bf16[16,16384]{1,0:T(8,128)(2,1)S(1)} %shard_map.69.refs_5_), channel_id=1, source_target_pairs={{0,1},{1,0},{2,3},{3,2},{4,5},{5,4},{6,7},{7,6},{8,9},{9,8},{10,11... | collective-permute-start | bytes 1572872 | tf_op jit(solution)/shard_map/ppermute | solution.py:312
  55.8 5.2 %collective-permute-start.16 = (bf16[16,16384]{1,0:T(8,128)(2,1)S(1)}, bf16[16,16384]{1,0:T(8,128)(2,1)S(1)}, u32[]{:S(2)}, u32[]{:S(2)}) collective-permute-start(bf16[16,16384]{1,0:T(8,128)(2,1)S(1)} %shard_map.70.refs_6_), channel_id=1, source_target_pairs={{0,1},{1,0},{2,3},{3,2},{4,5},{5,4},{6,7},{7,6},{8,9},{9,8},{10,11... | collective-permute-start | bytes 1572872 | tf_op jit(solution)/shard_map/ppermute | solution.py:312
  57.0 4.0 %collective-permute-start.17 = (bf16[16,16384]{1,0:T(8,128)(2,1)S(1)}, bf16[16,16384]{1,0:T(8,128)(2,1)S(1)}, u32[]{:S(2)}, u32[]{:S(2)}) collective-permute-start(bf16[16,16384]{1,0:T(8,128)(2,1)S(1)} %shard_map.73.refs_7_), channel_id=1, source_target_pairs={{0,1},{1,0},{2,3},{3,2},{4,5},{5,4},{6,7},{7,6},{8,9},{9,8},{10,11... | collective-permute-start | bytes 1572872 | tf_op jit(solution)/shard_map/ppermute | solution.py:312
  60.2 13.3 %collective-permute-start.13 = (bf16[16,128,128]{2,1,0:T(8,128)(2,1)S(1)}, bf16[16,128,128]{2,1,0:T(8,128)(2,1)S(1)}, u32[]{:S(2)}, u32[]{:S(2)}) collective-permute-start(bf16[16,128,128]{2,1,0:T(8,128)(2,1)S(1)} %get-tuple-element.52), channel_id=1, source_target_pairs={{0,1},{1,0},{2,3},{3,2},{4,5},{5,4},{6,7},{7,6},{8,9},{9,8},{10,11... | collective-permute-start | bytes 1572872 | tf_op jit(solution)/shard_map/ppermute | solution.py:312
  67.3 9.2 %collective-permute-start.18 = (bf16[2,32,640]{2,1,0:T(8,128)(2,1)S(1)}, bf16[2,32,640]{2,1,0:T(8,128)(2,1)S(1)}, u32[]{:S(2)}, u32[]{:S(2)}) collective-permute-start(bf16[2,32,640]{2,1,0:T(8,128)(2,1)S(1)} %get-tuple-element.57), channel_id=1, source_target_pairs={{0,16},{16,0},{32,48},{48,32},{64,80},{80,64},{96,112},{112,96},{1... | collective-permute-start | bytes 245768 | tf_op jit(solution)/shard_map/ppermute | solution.py:353
  68.8 9.3 %collective-permute-start.19 = (bf16[2,32,640]{2,1,0:T(8,128)(2,1)S(1)}, bf16[2,32,640]{2,1,0:T(8,128)(2,1)S(1)}, u32[]{:S(2)}, u32[]{:S(2)}) collective-permute-start(bf16[2,32,640]{2,1,0:T(8,128)(2,1)S(1)} %get-tuple-element.58), channel_id=1, source_target_pairs={{0,32},{16,48},{32,64},{48,80},{64,96},{80,112},{96,0},{112,16},{1... | collective-permute-start | bytes 245768 | tf_op jit(solution)/shard_map/ppermute | solution.py:353
  70.4 8.1 %collective-permute-start.20 = (bf16[2,32,640]{2,1,0:T(8,128)(2,1)S(1)}, bf16[2,32,640]{2,1,0:T(8,128)(2,1)S(1)}, u32[]{:S(2)}, u32[]{:S(2)}) collective-permute-start(bf16[2,32,640]{2,1,0:T(8,128)(2,1)S(1)} %get-tuple-element.59), channel_id=1, source_target_pairs={{0,48},{16,32},{32,80},{48,64},{64,112},{80,96},{96,16},{112,0},{1... | collective-permute-start | bytes 245768 | tf_op jit(solution)/shard_map/ppermute | solution.py:353
  72.0 8.7 %collective-permute-start.21 = (bf16[2,32,640]{2,1,0:T(8,128)(2,1)S(1)}, bf16[2,32,640]{2,1,0:T(8,128)(2,1)S(1)}, u32[]{:S(2)}, u32[]{:S(2)}) collective-permute-start(bf16[2,32,640]{2,1,0:T(8,128)(2,1)S(1)} %get-tuple-element.60), channel_id=1, source_target_pairs={{0,64},{16,80},{32,96},{48,112},{64,0},{80,16},{96,32},{112,48},{1... | collective-permute-start | bytes 245768 | tf_op jit(solution)/shard_map/ppermute | solution.py:353
  73.5 7.2 %collective-permute-start.22 = (bf16[2,32,640]{2,1,0:T(8,128)(2,1)S(1)}, bf16[2,32,640]{2,1,0:T(8,128)(2,1)S(1)}, u32[]{:S(2)}, u32[]{:S(2)}) collective-permute-start(bf16[2,32,640]{2,1,0:T(8,128)(2,1)S(1)} %get-tuple-element.61), channel_id=1, source_target_pairs={{0,80},{16,64},{32,112},{48,96},{64,16},{80,0},{96,48},{112,32},{1... | collective-permute-start | bytes 245768 | tf_op jit(solution)/shard_map/ppermute | solution.py:353
  76.4 5.4 %collective-permute-start.23 = (bf16[2,32,640]{2,1,0:T(8,128)(2,1)S(1)}, bf16[2,32,640]{2,1,0:T(8,128)(2,1)S(1)}, u32[]{:S(2)}, u32[]{:S(2)}) collective-permute-start(bf16[2,32,640]{2,1,0:T(8,128)(2,1)S(1)} %get-tuple-element.62), channel_id=1, source_target_pairs={{0,96},{16,112},{32,0},{48,16},{64,32},{80,48},{96,64},{112,80},{1... | collective-permute-start | bytes 245768 | tf_op jit(solution)/shard_map/ppermute | solution.py:353
  78.1 5.3 %collective-permute-start.24 = (bf16[2,32,640]{2,1,0:T(8,128)(2,1)S(1)}, bf16[2,32,640]{2,1,0:T(8,128)(2,1)S(1)}, u32[]{:S(2)}, u32[]{:S(2)}) collective-permute-start(bf16[2,32,640]{2,1,0:T(8,128)(2,1)S(1)} %get-tuple-element.63), channel_id=1, source_target_pairs={{0,112},{16,96},{32,16},{48,0},{64,48},{80,32},{96,80},{112,64},{1... | collective-permute-start | bytes 245768 | tf_op jit(solution)/shard_map/ppermute | solution.py:353
  (2 other events, 21.3 us)
